TPU v7x, 512 devices: a whole 4x4x16 slice. The times are simulated.
512 devices in a mesh: ctx: 64 (over y_lo, z, core), head: 8 (over x, y_hi).
Axes of the slice: x: 4, y: 4 (y_hi: 2, y_lo: 2; y = y_hi * 2 + y_lo), z: 16, core: 2. Of those that a mesh axis runs over, the one named last changes fastest.
Arguments:
- queries: bfloat16 [65536, 8, 128], P('ctx', 'head'), may hold values from -6 to 6
- keys: bfloat16 [65536, 128], P('ctx'), may hold values from -6 to 6
- values: bfloat16 [65536, 128], P('ctx'), may hold values from -6 to 6
- outputs: bfloat16 [65536, 8, 128], P('ctx', 'head'), may hold values from -6 to 6
- out_grad: bfloat16 [65536, 8, 128], P('ctx', 'head'), may hold values from -16 to 16
- log_norm: float32 [8, 65536], P('head', 'ctx'), may hold values from 6 to 8
- span_ids: int32 [128], replicated, may hold values from 0 to 127, as said below
Outputs:
- query_grad: bfloat16 [65536, 8, 128], P('ctx', 'head')
- key_grad: bfloat16 [65536, 128], P(('ctx', 'head'))
- value_grad: bfloat16 [65536, 128], P(('ctx', 'head'))
Inputs may be any that keep to these rules, and one draw needn't show every extreme that they name: `span_ids`: a permutation of 0 to 127 in which blocks 2 k and 2 k + 1 hold two spans that sum to 127.
All inputs are finite; a program needn't handle non-finite values.
Results may differ from a plain program's by a relative error of at most 0.0065.
Values may be sent and summed in bfloat16 or wider, within the bound.
A program may use at most 64 MiB of HBM per device.

v0:
```python
import jax
import jax.numpy as jnp
from jax import lax
from jax.sharding import PartitionSpec as P

STEPS = 3


def shifted(block, axis, distance):
    devices = range(lax.axis_size(axis))
    route = [((i - distance) % len(devices), i) for i in devices]
    return lax.ppermute(block, axis, route)


def holder_places(span_ids, holder, span):
    pair = lax.dynamic_slice_in_dim(span_ids, holder * 2, 2, 0)
    offsets = jnp.arange(span, dtype=jnp.int32)
    return (pair[:, None] * span + offsets[None, :]).reshape(-1)


def tile_grads(
    query_rows,
    grad_rows,
    norm_rows,
    delta_rows,
    query_places,
    key_rows,
    value_rows,
    key_places,
    scale,
):
    rows = query_rows.shape[0]
    block = min(rows, 512)
    query_parts = []
    key_part = jnp.zeros(key_rows.shape, jnp.float32)
    value_part = jnp.zeros(value_rows.shape, jnp.float32)
    for index in range(rows // block):
        low = index * block
        q_block = query_rows[low : low + block]
        g_block = grad_rows[low : low + block]
        n_block = norm_rows[:, low : low + block]
        d_block = delta_rows[low : low + block]
        allowed = key_places[None, :] <= query_places[low : low + block, None]
        scores = (
            jnp.einsum("qhd,kd->hqk", q_block, key_rows, preferred_element_type=jnp.float32) * scale
        )
        prob = jnp.where(allowed[None], jnp.exp(scores - n_block[:, :, None]), 0.0)
        value_part = value_part + jnp.einsum(
            "hqk,qhd->kd", prob.astype(jnp.bfloat16), g_block, preferred_element_type=jnp.float32
        )
        dprob = jnp.einsum("qhd,kd->hqk", g_block, value_rows, preferred_element_type=jnp.float32)
        dscore = (prob * (dprob - d_block.T[:, :, None])).astype(jnp.bfloat16)
        query_parts.append(
            scale * jnp.einsum("hqk,kd->qhd", dscore, key_rows, preferred_element_type=jnp.float32)
        )
        key_part = key_part + scale * jnp.einsum(
            "hqk,qhd->kd", dscore, q_block, preferred_element_type=jnp.float32
        )
    return (jnp.concatenate(query_parts, axis=0), key_part, value_part)


def local(queries, keys, values, outputs, out_grad, log_norm, span_ids):
    tok_rows = queries.shape[0]
    span = tok_rows // 2
    scale = queries.shape[2] ** (-0.5)
    holders = lax.axis_size("ctx")
    myself = lax.axis_index("ctx")
    delta = jnp.sum(out_grad.astype(jnp.float32) * outputs.astype(jnp.float32), axis=2)
    my_places = holder_places(span_ids, myself, span)
    key_cur, value_cur = (keys, values)
    key_acc = jnp.zeros(keys.shape, jnp.float32)
    value_acc = jnp.zeros(values.shape, jnp.float32)
    query_acc = jnp.zeros(queries.shape, jnp.float32)
    for step in range(STEPS):
        if step > 0:
            key_cur, value_cur = shifted((key_cur, value_cur), "ctx", 1)
            key_acc, value_acc = shifted((key_acc, value_acc), "ctx", 1)
        key_places = holder_places(span_ids, (myself - step) % holders, span)
        query_part, key_part, value_part = tile_grads(
            queries, out_grad, log_norm, delta, my_places, key_cur, value_cur, key_places, scale
        )
        query_acc = query_acc + query_part
        key_acc = key_acc + key_part
        value_acc = value_acc + value_part
    key_acc, value_acc = shifted((key_acc, value_acc), "ctx", 1 - STEPS)
    key_sum, value_sum = (
        lax.psum_scatter(key_acc, "head", scatter_dimension=0, tiled=True),
        lax.psum_scatter(value_acc, "head", scatter_dimension=0, tiled=True),
    )
    return (
        query_acc.astype(jnp.bfloat16),
        key_sum.astype(jnp.bfloat16),
        value_sum.astype(jnp.bfloat16),
    )


def solution(mesh):
    in_specs = (
        P("ctx", "head", None),
        P("ctx", None),
        P("ctx", None),
        P("ctx", "head", None),
        P("ctx", "head", None),
        P("head", "ctx"),
        P(),
    )
    out_specs = (P("ctx", "head", None), P(("ctx", "head"), None), P(("ctx", "head"), None))
    return jax.shard_map(local, mesh=mesh, in_specs=in_specs, out_specs=out_specs, check_vma=False)
```

profile of v0, /device:TPU:1, one launch (start us, length us, event | category | flops | bytes accessed | tf_op | source)
XLA Modules:
  0.0 251.8 jit_solution(11108536421632369981)
XLA Ops:
  7.2 0.0 reduce-scatter.3.cloned.1.call-start
  7.2 5.1 %collective-permute-start.1 = (bf16[1024,128]{1,0:T(8,128)(2,1)}, bf16[1024,128]{1,0:T(8,128)(2,1)}, u32[]{:S(2)}, u32[]{:S(2)}) collective-permute-start(bf16[1024,128]{1,0:T(8,128)(2,1)} %param.9), channel_id=1, source_target_pairs={{504,0},{0,8},{8,16},{16,24},{24,32},{32,40},{40,48},{48,56},{56,6... | collective-permute-start | bytes 786440 | tf_op jit(solution)/shard_map/ppermute | solution.py:12
  12.3 1.9 collective-permute-start
  14.3 0.9 dynamic-slice_multiply_fusion
  15.2 0.1 iota_add_fusion
  15.3 0.1 add_bitcast_fusion.2
  15.3 1.2 multiply_reduce_fusion
  16.6 0.7 fusion.99
  17.3 1.6 bitcast_select_fusion.5
  18.9 0.4 fusion.12
  19.4 0.5 copy-done.10
  19.8 0.4 fusion.68
  20.3 0.6 bitcast_select_fusion.4
  20.9 0.4 fusion.13
  21.3 0.4 fusion.18
  21.7 3.9 %collective-permute-start.4 = (f32[1024,128]{1,0:T(8,128)S(1)}, f32[1024,128]{1,0:T(8,128)S(1)}, u32[]{:S(2)}, u32[]{:S(2)}) collective-permute-start(f32[1024,128]{1,0:T(8,128)S(1)} %fusion.18), channel_id=1, source_target_pairs={{504,0},{0,8},{8,16},{16,24},{24,32},{32,40},{40,48},{48,56},{56,6... | collective-permute-start | bytes 1572872 | tf_op jit(solution)/shard_map/ppermute | solution.py:12
  25.7 0.4 fusion.36
  26.1 0.4 convolution_add_fusion.2
  26.6 1.9 collective-permute-start.7
  28.5 0.1 add_bitcast_fusion
  28.6 3.9 %collective-permute-start.2 = (bf16[1024,128]{1,0:T(8,128)(2,1)}, bf16[1024,128]{1,0:T(8,128)(2,1)S(1)}, u32[]{:S(2)}, u32[]{:S(2)}) collective-permute-start(bf16[1024,128]{1,0:T(8,128)(2,1)} %collective-permute-done), channel_id=1, source_target_pairs={{504,0},{0,8},{8,16},{16,24},{24,32},{32,40},{40,48},{48,56},{56,6... | collective-permute-start | bytes 786440 | tf_op jit(solution)/shard_map/ppermute | solution.py:12
  32.5 1.5 bitcast_select_fusion.2
  34.1 1.5 bitcast_select_fusion.3
  35.6 1.9 collective-permute-start.3
  37.5 1.4 fusion.15
  39.0 1.6 fusion.14
  40.5 0.4 fusion.66
  41.0 0.5 fusion.20
  41.5 5.1 %collective-permute-start.5 = (f32[1024,128]{1,0:T(8,128)S(1)}, f32[1024,128]{1,0:T(8,128)S(1)}, u32[]{:S(2)}, u32[]{:S(2)}) collective-permute-start(f32[1024,128]{1,0:T(8,128)S(1)} %fusion.20), channel_id=1, source_target_pairs={{504,0},{0,8},{8,16},{16,24},{24,32},{32,40},{40,48},{48,56},{56,6... | collective-permute-start | bytes 1572872 | tf_op jit(solution)/shard_map/ppermute | solution.py:12
  46.6 0.6 bitcast_select_fusion
  47.2 0.6 bitcast_select_fusion.1
  47.8 0.4 fusion.17
  48.3 0.3 copy-done.7
  48.5 0.4 fusion.16
  49.0 0.2 copy-done.9
  49.2 0.4 fusion.64
  49.6 0.4 fusion.21
  50.1 2.6 %collective-permute-done.5 = f32[1024,128]{1,0:T(8,128)S(1)} collective-permute-done((f32[1024,128]{1,0:T(8,128)S(1)}, f32[1024,128]{1,0:T(8,128)S(1)}, u32[]{:S(2)}, u32[]{:S(2)}) %collective-permute-start.5) | collective-permute-done | bytes 524320 | tf_op jit(solution)/shard_map/ppermute | solution.py:12
  52.7 0.1 add.181
  52.8 3.9 %collective-permute-start.6 = (f32[1024,128]{1,0:T(8,128)S(1)}, f32[1024,128]{1,0:T(8,128)}, u32[]{:S(2)}, u32[]{:S(2)}) collective-permute-start(f32[1024,128]{1,0:T(8,128)S(1)} %add.181), channel_id=1, source_target_pairs={{16,0},{24,8},{32,16},{40,24},{48,32},{56,40},{64,48},{72,56},{80,... | collective-permute-start | bytes 1572872 | tf_op jit(solution)/shard_map/ppermute | solution.py:12
  56.7 0.4 fusion.33
  57.1 1.3 fusion.22
  58.4 4.7 %collective-permute-start.8 = (f32[1024,128]{1,0:T(8,128)}, f32[1024,128]{1,0:T(8,128)}, u32[]{:S(2)}, u32[]{:S(2)}) collective-permute-start(f32[1024,128]{1,0:T(8,128)} %fusion.22), channel_id=1, source_target_pairs={{504,0},{0,8},{8,16},{16,24},{24,32},{32,40},{40,48},{48,56},{56,6... | collective-permute-start | bytes 1572872 | tf_op jit(solution)/shard_map/ppermute | solution.py:12
  63.1 2.4 collective-permute-done.6
  65.4 0.0 reduce-scatter.3.cloned.1.call-update
  65.5 0.0 reduce-scatter.5.cloned.1.call-start
  65.5 2.2 fusion.30
  67.7 0.0 copy-done.8
  67.7 0.4 convolution_add_fusion
  68.2 1.3 collective-permute-done.8
  69.5 1.1 add.186
  70.6 6.2 %collective-permute-start.9 = (f32[1024,128]{1,0:T(8,128)S(1)}, f32[1024,128]{1,0:T(8,128)}, u32[]{:S(2)}, u32[]{:S(2)}) collective-permute-start(f32[1024,128]{1,0:T(8,128)S(1)} %add.186), channel_id=1, source_target_pairs={{16,0},{24,8},{32,16},{40,24},{48,32},{56,40},{64,48},{72,56},{80,... | collective-permute-start | bytes 1572872 | tf_op jit(solution)/shard_map/ppermute | solution.py:12
  76.8 8.7 %collective-permute-done.9 = f32[1024,128]{1,0:T(8,128)} collective-permute-done((f32[1024,128]{1,0:T(8,128)S(1)}, f32[1024,128]{1,0:T(8,128)}, u32[]{:S(2)}, u32[]{:S(2)}) %collective-permute-start.9) | collective-permute-done | bytes 524320 | tf_op jit(solution)/shard_map/ppermute | solution.py:12
  85.5 1.5 fusion.27
  87.1 1.5 fusion.28
  88.6 1.5 fusion.25
  90.1 1.4 fusion.26
  91.6 0.5 fusion.23
  92.1 0.5 fusion.24
  92.6 0.8 fusion.45
  93.3 59.9 %reduce-scatter.3.cloned.1.call-done = f32[128,128]{1,0:T(8,128)} async-done(((f32[1024,128]{1,0:T(8,128)}), f32[128,128]{1,0:T(8,128)}) %reduce-scatter.3.cloned.1.call-update) | async-done | bytes 65552 | tf_op jit(solution)/shard_map/reduce_scatter | solution.py:87
  153.2 1.5 convert_element_type.68
  154.7 88.9 %reduce-scatter.5.cloned.1.call-done = f32[128,128]{1,0:T(8,128)} async-done(((f32[1024,128]{1,0:T(8,128)}), f32[128,128]{1,0:T(8,128)}) %reduce-scatter.5.cloned.1.call-update) | async-done | bytes 65552 | tf_op jit(solution)/shard_map/reduce_scatter | solution.py:88
  243.5 1.5 convert_element_type.75
  (38 shorter events, 0.1 us)
Async XLA Ops:
  7.2 11.7 %copy-start.11 = (bf16[1024,128]{1,0:T(8,128)(2,1)S(1)}, bf16[1024,128]{1,0:T(8,128)(2,1)}, u32[]{:S(2)}) copy-start(bf16[1024,128]{1,0:T(8,128)(2,1)} %param.9) | copy-start | bytes 786436
  7.2 11.7 %copy-start = (bf16[1024,1,128]{2,0,1:T(8,128)(2,1)S(1)}, bf16[1024,1,128]{2,0,1:T(8,128)(2,1)}, u32[]{:S(2)}) copy-start(bf16[1024,1,128]{2,0,1:T(8,128)(2,1)} %param.11) | copy-start | bytes 786436
  7.2 146.0 %reduce-scatter.3.cloned.1.call-start = ((), (), s32[]{:S(2)}) async-start(), calls=%async_computation.2 | async-start | bytes 589824 | tf_op jit(solution)/shard_map/reduce_scatter | solution.py:87
  7.2 28.4 %collective-permute-start.1 = (bf16[1024,128]{1,0:T(8,128)(2,1)}, bf16[1024,128]{1,0:T(8,128)(2,1)}, u32[]{:S(2)}, u32[]{:S(2)}) collective-permute-start(bf16[1024,128]{1,0:T(8,128)(2,1)} %param.9), channel_id=1, source_target_pairs={{504,0},{0,8},{8,16},{16,24},{24,32},{32,40},{40,48},{48,56},{56,6... | collective-permute-start | bytes 786440 | tf_op jit(solution)/shard_map/ppermute | solution.py:12
  12.3 16.3 %collective-permute-start = (bf16[1024,128]{1,0:T(8,128)(2,1)}, bf16[1024,128]{1,0:T(8,128)(2,1)}, u32[]{:S(2)}, u32[]{:S(2)}) collective-permute-start(bf16[1024,128]{1,0:T(8,128)(2,1)} %param.8), channel_id=1, source_target_pairs={{504,0},{0,8},{8,16},{16,24},{24,32},{32,40},{40,48},{48,56},{56,6... | collective-permute-start | bytes 786440 | tf_op jit(solution)/shard_map/ppermute | solution.py:12
  18.9 1.0 copy-start.10
  18.9 1.4 copy-start.12
  21.7 19.2 %collective-permute-start.4 = (f32[1024,128]{1,0:T(8,128)S(1)}, f32[1024,128]{1,0:T(8,128)S(1)}, u32[]{:S(2)}, u32[]{:S(2)}) collective-permute-start(f32[1024,128]{1,0:T(8,128)S(1)} %fusion.18), channel_id=1, source_target_pairs={{504,0},{0,8},{8,16},{16,24},{24,32},{32,40},{40,48},{48,56},{56,6... | collective-permute-start | bytes 1572872 | tf_op jit(solution)/shard_map/ppermute | solution.py:12
  26.6 30.5 %collective-permute-start.7 = (f32[1024,128]{1,0:T(8,128)S(1)}, f32[1024,128]{1,0:T(8,128)S(1)}, u32[]{:S(2)}, u32[]{:S(2)}) collective-permute-start(f32[1024,128]{1,0:T(8,128)S(1)} %convolution_add_fusion.2), channel_id=1, source_target_pairs={{504,0},{0,8},{8,16},{16,24},{24,32},{32,40},{40,48},{48,56},{56,6... | collective-permute-start | bytes 1572872 | tf_op jit(solution)/shard_map/ppermute | solution.py:12
  28.6 18.0 %collective-permute-start.2 = (bf16[1024,128]{1,0:T(8,128)(2,1)}, bf16[1024,128]{1,0:T(8,128)(2,1)S(1)}, u32[]{:S(2)}, u32[]{:S(2)}) collective-permute-start(bf16[1024,128]{1,0:T(8,128)(2,1)} %collective-permute-done), channel_id=1, source_target_pairs={{504,0},{0,8},{8,16},{16,24},{24,32},{32,40},{40,48},{48,56},{56,6... | collective-permute-start | bytes 786440 | tf_op jit(solution)/shard_map/ppermute | solution.py:12
  35.6 12.2 %collective-permute-start.3 = (bf16[1024,128]{1,0:T(8,128)(2,1)}, bf16[1024,128]{1,0:T(8,128)(2,1)S(1)}, u32[]{:S(2)}, u32[]{:S(2)}) collective-permute-start(bf16[1024,128]{1,0:T(8,128)(2,1)} %collective-permute-done.1), channel_id=1, source_target_pairs={{504,0},{0,8},{8,16},{16,24},{24,32},{32,40},{40,48},{48,56},{56,6... | collective-permute-start | bytes 786440 | tf_op jit(solution)/shard_map/ppermute | solution.py:12
  38.9 2.0 copy-start.1
  41.5 11.2 %collective-permute-start.5 = (f32[1024,128]{1,0:T(8,128)S(1)}, f32[1024,128]{1,0:T(8,128)S(1)}, u32[]{:S(2)}, u32[]{:S(2)}) collective-permute-start(f32[1024,128]{1,0:T(8,128)S(1)} %fusion.20), channel_id=1, source_target_pairs={{504,0},{0,8},{8,16},{16,24},{24,32},{32,40},{40,48},{48,56},{56,6... | collective-permute-start | bytes 1572872 | tf_op jit(solution)/shard_map/ppermute | solution.py:12
  46.6 1.2 copy-start.13
  47.2 1.3 copy-start.7
  47.8 1.4 copy-start.9
  48.5 1.1 copy-start.5
  49.2 3.6 %copy-start.3 = (bf16[512,1024]{0,1:T(8,128)(2,1)}, bf16[512,1024]{0,1:T(8,128)(2,1)S(1)}, u32[]{:S(2)}) copy-start(bf16[512,1024]{0,1:T(8,128)(2,1)S(1)} %fusion.16) | copy-start | bytes 3145732
  52.8 12.7 %collective-permute-start.6 = (f32[1024,128]{1,0:T(8,128)S(1)}, f32[1024,128]{1,0:T(8,128)}, u32[]{:S(2)}, u32[]{:S(2)}) collective-permute-start(f32[1024,128]{1,0:T(8,128)S(1)} %add.181), channel_id=1, source_target_pairs={{16,0},{24,8},{32,16},{40,24},{48,32},{56,40},{64,48},{72,56},{80,... | collective-permute-start | bytes 1572872 | tf_op jit(solution)/shard_map/ppermute | solution.py:12
  58.4 11.1 %collective-permute-start.8 = (f32[1024,128]{1,0:T(8,128)}, f32[1024,128]{1,0:T(8,128)}, u32[]{:S(2)}, u32[]{:S(2)}) collective-permute-start(f32[1024,128]{1,0:T(8,128)} %fusion.22), channel_id=1, source_target_pairs={{504,0},{0,8},{8,16},{16,24},{24,32},{32,40},{40,48},{48,56},{56,6... | collective-permute-start | bytes 1572872 | tf_op jit(solution)/shard_map/ppermute | solution.py:12
  65.5 178.1 %reduce-scatter.5.cloned.1.call-start = ((), (), s32[]{:S(2)}) async-start(), calls=%async_computation.3 | async-start | bytes 589824 | tf_op jit(solution)/shard_map/reduce_scatter | solution.py:88
  65.5 2.2 copy-start.8
  70.6 14.9 %collective-permute-start.9 = (f32[1024,128]{1,0:T(8,128)S(1)}, f32[1024,128]{1,0:T(8,128)}, u32[]{:S(2)}, u32[]{:S(2)}) collective-permute-start(f32[1024,128]{1,0:T(8,128)S(1)} %add.186), channel_id=1, source_target_pairs={{16,0},{24,8},{32,16},{40,24},{48,32},{56,40},{64,48},{72,56},{80,... | collective-permute-start | bytes 1572872 | tf_op jit(solution)/shard_map/ppermute | solution.py:12
  85.5 3.1 %copy-start.2 = (bf16[512,1024]{0,1:T(8,128)(2,1)S(1)}, bf16[512,1024]{0,1:T(8,128)(2,1)}, u32[]{:S(2)}) copy-start(bf16[512,1024]{0,1:T(8,128)(2,1)} %copy-done.1) | copy-start | bytes 3145732
  87.0 4.5 %copy-start.6 = (bf16[512,1024]{0,1:T(8,128)(2,1)S(1)}, bf16[512,1024]{0,1:T(8,128)(2,1)}, u32[]{:S(2)}) copy-start(bf16[512,1024]{0,1:T(8,128)(2,1)} %copy-done.5) | copy-start | bytes 3145732
  87.1 4.5 %copy-start.14 = (bf16[1024,128]{1,0:T(8,128)(2,1)S(1)}, bf16[1024,128]{1,0:T(8,128)(2,1)}, u32[]{:S(2)}) copy-start(bf16[1024,128]{1,0:T(8,128)(2,1)} %copy-done.13) | copy-start | bytes 786436
  88.6 3.5 %copy-start.4 = (bf16[512,1024]{0,1:T(8,128)(2,1)S(1)}, bf16[512,1024]{0,1:T(8,128)(2,1)}, u32[]{:S(2)}) copy-start(bf16[512,1024]{0,1:T(8,128)(2,1)} %copy-done.3) | copy-start | bytes 3145732
Sparse Core Ops, SparseCore 0:
  65.6 87.5 reduce-scatter.2
  158.3 85.1 reduce-scatter.4
where the time goes:
time: 253 us; the launch traced here: 252 us
  waiting for transfers between devices  164 us (65%)
  starting transfers between devices  38.7 us (15%)
  matrix products  25.8 us (10%)
  between operations  14.6 us (6%)
  other arithmetic  7.19 us (3%)
    reduce_scatter x1, waiting for transfers between devices, local(): lax.psum_scatter(value_acc, 'head', scatter_dimension=0, tiled=True)  88.9 us
    reduce_scatter x1, waiting for transfers between devices, local(): lax.psum_scatter(key_acc, 'head', scatter_dimension=0, tiled=True)  59.9 us
    ppermute x10, starting transfers between devices, shifted(): return lax.ppermute(block, axis, route)  38.6 us
    ppermute x10, waiting for transfers between devices, shifted(): return lax.ppermute(block, axis, route)  15 us
    dot_general x6, matrix products, tile_grads(): jnp.einsum('hqk,kd->qhd', dscore, key_rows, preferred_element_type=jnp.fl...  6.93 us
    dot_general x6, matrix products, tile_grads(): jnp.einsum('qhd,kd->hqk', q_block, key_rows, preferred_element_type=jnp.f...  6.41 us
    dot_general x6, matrix products, tile_grads(): jnp.einsum('hqk,qhd->kd', prob.astype(jnp.bfloat16), g_block, preferred_e...  5.19 us
  transfers between devices with their start and end apart: 12, of which 6 were waited for; matrix products, arithmetic and copies ran while one was open for 13% of the time, Pallas kernels for 0%

commit v1 on v0

v1 whole, which is shorter than its diff:
```python
import jax
import jax.numpy as jnp
from jax import lax
from jax.experimental import pallas as pl
from jax.experimental.pallas import tpu as pltpu
from jax.sharding import PartitionSpec as P

MESH = pl.DeviceIdType.MESH
F32 = jnp.float32
BF16 = jnp.bfloat16
LOG2E = 1.4426950408889634
NT = (((1,), (1,)), ((), ()))
TN = (((0,), (0,)), ((), ()))
SPAN = 512
TOK = 2 * SPAN
DIM = 128
SCALE = DIM ** -0.5


def tile(q, g, norm, delta, k, v, diagonal=False):
    score = lax.dot_general(k, q, NT, preferred_element_type=F32)
    prob = jnp.exp2(score * (SCALE * LOG2E) - norm)
    if diagonal:
        rows = lax.broadcasted_iota(jnp.int32, score.shape, 0)
        prob = jnp.where(rows <= lax.broadcasted_iota(jnp.int32, score.shape, 1), prob, 0.0)
    dprob = lax.dot_general(v, g, NT, preferred_element_type=F32)
    dscore = (prob * (dprob - delta)).astype(BF16)
    dv = jnp.dot(prob.astype(BF16), g, preferred_element_type=F32)
    dk = jnp.dot(dscore, q, preferred_element_type=F32)
    dq = lax.dot_general(dscore, k, TN, preferred_element_type=F32)
    return dq, dk, dv


def kernel(
    holders, heads, span_ref, q_in, g_in, o_in, k_in, v_in, norm_in, dq_out, dk_out, dv_out,
    raw_q, raw_g, raw_k, raw_v, raw_o, q_own, q_far, kv_own, kv_mate, kv_far,
    norm_own, norm_far, delta_own, delta_far, dq_acc, dk_acc, dv_acc, dq_end, dk_end, dv_end,
    mate_out, mate_part, next_out, dq_part, back_out, back_part, own_out, own_part,
    load_sem, kv_sem, mate_sem, far_sem, row_sem, dq_sem, back_send, back_recv, own_send, own_recv, ready,
):
    c = lax.axis_index("ctx")
    h = lax.axis_index("head")
    side = lax.rem(c, 2)
    even, odd = side == 0, side == 1
    mate = {"ctx": c + 1 - 2 * side}
    ahead = lax.rem(c + 2, holders)
    behind = lax.rem(c + holders - 2, holders)

    loads = [
        pltpu.make_async_copy(ref, raw, load_sem.at[i])
        for i, (ref, raw) in enumerate(
            ((q_in, raw_q), (g_in, raw_g), (k_in, raw_k), (v_in, raw_v), (o_in, raw_o))
        )
    ]
    for copy in loads:
        copy.start()

    barrier = pltpu.get_barrier_semaphore()
    pl.semaphore_signal(barrier, inc=1, device_id=mate, device_id_type=MESH)
    pl.semaphore_signal(barrier, inc=1, device_id={"ctx": behind}, device_id_type=MESH)
    for step in range(1, heads):
        pl.semaphore_signal(
            barrier, inc=1, device_id={"head": lax.rem(h + step, heads)}, device_id_type=MESH
        )

    def first(holder):
        return span_ref[2 * holder]

    def second(holder):
        return span_ref[2 * holder + 1]

    def low_span(holder):
        return jnp.minimum(first(holder), second(holder))

    def late(holder):
        return (first(holder) > second(holder)).astype(jnp.int32)

    low_place = late(c)
    asks = jnp.where(even, ahead, c)
    lows = [
        (low_span(c + 1 - 2 * side) < low_span(asks)).astype(jnp.int32),
        (low_span(jnp.where(even, c, behind)) < low_span(asks)).astype(jnp.int32),
    ]

    lo, hi = low_place * SPAN, (1 - low_place) * SPAN
    for copy in loads[:4]:
        copy.wait()
    for i, (raw, place) in enumerate(((raw_q, hi), (raw_g, hi), (raw_q, lo), (raw_g, lo))):
        q_own[pl.ds(i * SPAN, SPAN)] = raw[pl.ds(place, SPAN)]
    for i, (raw, place) in enumerate(((raw_k, lo), (raw_v, lo), (raw_k, hi), (raw_v, hi))):
        kv_own[pl.ds(i * SPAN, SPAN)] = raw[pl.ds(place, SPAN)]
    loads[4].wait()
    for i, place in enumerate((hi, lo)):
        norm_own[:, pl.ds(i * SPAN, SPAN)] = norm_in[:, pl.ds(place, SPAN)] * LOG2E
        product = raw_g[pl.ds(place, SPAN)].astype(F32) * raw_o[pl.ds(place, SPAN)].astype(F32)
        delta_own[:, pl.ds(i * SPAN, SPAN)] = jnp.sum(product.T, axis=0, keepdims=True)

    pl.semaphore_wait(barrier, heads + 1)

    def remote(src, dst, send, recv, device):
        return pltpu.make_async_remote_copy(
            src_ref=src, dst_ref=dst, send_sem=send, recv_sem=recv, device_id=device, device_id_type=MESH
        )

    half = lambda i: pl.ds(i * TOK, TOK)
    kv_copy = remote(kv_own, kv_mate, kv_sem.at[0], kv_sem.at[1], mate)
    q_copies = [
        remote(q_own.at[half(i)], q_far.at[half(i)], far_sem.at[0, i], far_sem.at[1, i], {"ctx": behind})
        for i in range(2)
    ]
    row_copies = [
        remote(own, far, row_sem.at[0, i], row_sem.at[1, i], {"ctx": behind})
        for i, (own, far) in enumerate(((norm_own, norm_far), (delta_own, delta_far)))
    ]
    back_copies = [
        remote(kv_own.at[half(i)], kv_far.at[half(i)], far_sem.at[0, i], far_sem.at[1, i], {"ctx": ahead})
        for i in range(2)
    ]

    kv_copy.start()

    @pl.when(odd)
    def _():
        for copy in back_copies:
            copy.start()

    @pl.when(even)
    def _():
        pl.semaphore_signal(ready, inc=1, device_id={"ctx": ahead}, device_id_type=MESH)
        pl.semaphore_wait(ready, 1)
        for copy in (*row_copies, *q_copies):
            copy.start()

    def either(a, b):
        return a + b - 2 * a * b

    def at(i, size):
        return pl.ds(i * size, size)

    def block(qslot, qpart, kvslot, kvpart, diagonal=False):
        q, norm, delta = ((q_own, norm_own, delta_own), (q_far, norm_far, delta_far))[qslot]
        kv = (kv_own, kv_mate, kv_far)[kvslot]
        return tile(
            q[at(2 * qpart, SPAN)],
            q[at(2 * qpart + 1, SPAN)],
            norm[:, at(qpart, SPAN)],
            delta[:, at(qpart, SPAN)],
            kv[at(2 * kvpart, SPAN)],
            kv[at(2 * kvpart + 1, SPAN)],
            diagonal,
        )

    def crossing(qslot, kvslot, new_q, new_kv):
        dq, dk, dv = block(qslot, 0, kvslot, 0)
        top = pl.ds(0, SPAN)
        dq_acc[qslot, top] = dq if new_q else dq_acc[qslot, top] + dq
        dk_acc[kvslot, top] = dk if new_kv else dk_acc[kvslot, top] + dk
        dv_acc[kvslot, top] = dv if new_kv else dv_acc[kvslot, top] + dv

    def level(pair, qslot, kvslot):
        dq, dk, dv = block(qslot, lows[pair], kvslot, 1 - lows[pair])
        top = pl.ds(0, SPAN)
        dq_end[pair, top] = dq
        dk_end[pair, top] = dk
        dv_end[pair, top] = dv

    crossing(0, 0, True, True)
    dq, dk, dv = block(0, 1, 0, 0, True)
    dq_acc[0, pl.ds(SPAN, SPAN)] = dq
    dk_acc[0, pl.ds(0, SPAN)] += dk
    dv_acc[0, pl.ds(0, SPAN)] += dv
    dq, dk, dv = block(0, 0, 0, 1, True)
    dq_acc[0, pl.ds(0, SPAN)] += dq
    dk_acc[0, pl.ds(SPAN, SPAN)] = dk
    dv_acc[0, pl.ds(SPAN, SPAN)] = dv

    for ref in (dk_acc, dv_acc):
        for slot in (1, 2):
            ref[slot, pl.ds(SPAN, SPAN)] = jnp.zeros((SPAN, DIM), F32)
    for ref in (dq_end, dk_end, dv_end):
        for pair in range(2):
            ref[pair, pl.ds(SPAN, SPAN)] = jnp.zeros((SPAN, DIM), F32)

    def if_low(pair, part, end, on=1):
        return end[pair, at(1 - on * either(lows[pair], part), SPAN)]

    mate_copy = remote(mate_out, mate_part, mate_sem.at[0], mate_sem.at[1], mate)

    def send_mate():
        for part in range(2):
            for i, (acc, end, factor) in enumerate(((dk_acc, dk_end, SCALE), (dv_acc, dv_end, 1.0))):
                value = if_low(0, part, end)
                if part == 0:
                    value += acc[1, pl.ds(0, SPAN)]
                mate_out[pl.ds(part * TOK + i * SPAN, SPAN)] = (value * factor).astype(BF16)
        mate_copy.start()

    dq_copy = remote(next_out, dq_part, dq_sem.at[0], dq_sem.at[1], {"ctx": ahead})
    back_sends = [
        remote(
            back_out.at[to], back_part.at[h], back_send.at[to], back_recv.at[h], {"ctx": behind, "head": to}
        )
        for to in range(heads)
    ]

    @pl.when(even)
    def _():
        kv_copy.wait_recv()
        for copy in row_copies:
            copy.wait_recv()
        q_copies[0].wait_recv()
        crossing(1, 1, True, True)
        crossing(1, 0, False, False)
        q_copies[1].wait_recv()
        level(0, 1, 1)
        send_mate()
        level(1, 1, 0)
        for part in range(2):
            value = if_low(0, 1 - part, dq_end) + if_low(1, 1 - part, dq_end)
            if part == 0:
                value += dq_acc[1, pl.ds(0, SPAN)]
            next_out[pl.ds(part * SPAN, SPAN)] = (value * SCALE).astype(BF16)
        dq_copy.start()

    low_of = [low_place, 1 - low_place]

    @pl.when(odd)
    def _():
        kv_copy.wait_recv()
        crossing(0, 1, False, True)
        level(0, 0, 1)
        send_mate()
        back_copies[0].wait_recv()
        crossing(0, 2, False, True)
        back_copies[1].wait_recv()
        level(1, 0, 2)
        place = late(behind)
        for p in range(2):
            part = either(place, p)
            for i, (acc, end, factor) in enumerate(((dk_acc, dk_end, SCALE), (dv_acc, dv_end, 1.0))):
                value = if_low(1, part, end) + acc[2, at(part, SPAN)]
                value = (value * factor).astype(BF16)
                each = TOK // heads
                for s in range(heads // 2):
                    back_out[p * (heads // 2) + s, pl.ds(i * each, each)] = value[s * each : (s + 1) * each]
        for copy in back_sends:
            copy.start()

    mate_copy.wait_recv()
    each = TOK // heads
    for p in range(2):
        part = low_of[p]
        for i, (acc, end, factor) in enumerate(((dk_acc, dk_end, SCALE), (dv_acc, dv_end, 1.0))):
            value = (acc[0, at(part, SPAN)] + if_low(1, part, end, 1 - side)) * factor
            value += mate_part[at(2 * part + i, SPAN)].astype(F32)
            value = value.astype(BF16)
            for s in range(heads // 2):
                own_out[p * (heads // 2) + s, pl.ds(i * each, each)] = value[s * each : (s + 1) * each]
    own_sends = []
    for step in range(1, heads):
        to = lax.rem(h + step, heads)
        own_sends.append(remote(own_out.at[to], own_part.at[h], own_send.at[to], own_recv.at[h], {"head": to}))
        own_sends[-1].start()
    own_part[h] = own_out[h]

    @pl.when(even)
    def _():
        dq_copy.wait_recv()
        for p in range(2):
            place = (1 - low_of[p]) * SPAN
            value = dq_acc[0, pl.ds(place, SPAN)] * SCALE + dq_part[pl.ds(place, SPAN)].astype(F32)
            dq_out[pl.ds(p * SPAN, SPAN)] = value.astype(BF16)

    @pl.when(odd)
    def _():
        for p in range(2):
            place = (1 - low_of[p]) * SPAN
            value = dq_acc[0, pl.ds(place, SPAN)]
            value += if_low(0, low_of[p], dq_end) + if_low(1, low_of[p], dq_end)
            dq_out[pl.ds(p * SPAN, SPAN)] = (value * SCALE).astype(BF16)

    for step in range(1, heads):
        sender = lax.rem(h + step, heads)
        remote(own_out.at[sender], own_part.at[sender], own_send.at[sender], own_recv.at[sender], mate).wait_recv()
    total = own_part[0].astype(F32)
    for i in range(1, heads):
        total += own_part[i].astype(F32)
    dk_out[...] = total[:each].astype(BF16)
    dv_out[...] = total[each:].astype(BF16)

    @pl.when(odd)
    def _():
        for i in range(heads):
            remote(back_out.at[i], back_part.at[i], back_send.at[i], back_recv.at[i], mate).wait_recv()
        more = total
        for i in range(heads):
            more += back_part[i].astype(F32)
        dk_out[...] = more[:each].astype(BF16)
        dv_out[...] = more[each:].astype(BF16)

    kv_copy.wait_send()
    mate_copy.wait_send()
    for copy in own_sends:
        copy.wait_send()

    @pl.when(even)
    def _():
        for copy in (*row_copies, *q_copies, dq_copy):
            copy.wait_send()

    @pl.when(odd)
    def _():
        for copy in (*back_copies, *back_sends):
            copy.wait_send()


def local(queries, keys, values, outputs, out_grad, log_norm, span_ids):
    holders, heads = lax.axis_size("ctx"), lax.axis_size("head")
    each = TOK // heads
    flat = lambda a: a.reshape(TOK, DIM)
    body = lambda *refs: kernel(holders, heads, *refs)
    dma = pltpu.SemaphoreType.DMA
    dq, dk, dv = pl.pallas_call(
        body,
        out_shape=[
            jax.ShapeDtypeStruct((TOK, DIM), BF16),
            jax.ShapeDtypeStruct((each, DIM), BF16),
            jax.ShapeDtypeStruct((each, DIM), BF16),
        ],
        in_specs=[
            pl.BlockSpec(memory_space=pltpu.SMEM),
            *[pl.BlockSpec(memory_space=pl.ANY)] * 5,
            pl.BlockSpec(memory_space=pltpu.VMEM),
        ],
        out_specs=[pl.BlockSpec(memory_space=pltpu.VMEM)] * 3,
        scratch_shapes=[
            *[pltpu.VMEM((TOK, DIM), BF16)] * 5,
            *[pltpu.VMEM((2 * TOK, DIM), BF16)] * 5,
            *[pltpu.VMEM((1, TOK), F32)] * 4,
            pltpu.VMEM((2, TOK, DIM), F32),
            pltpu.VMEM((3, TOK, DIM), F32),
            pltpu.VMEM((3, TOK, DIM), F32),
            pltpu.VMEM((2, TOK, DIM), F32),
            pltpu.VMEM((2, TOK, DIM), F32),
            pltpu.VMEM((2, TOK, DIM), F32),
            pltpu.VMEM((2 * TOK, DIM), BF16),
            pltpu.VMEM((2 * TOK, DIM), BF16),
            pltpu.VMEM((TOK, DIM), BF16),
            pltpu.VMEM((TOK, DIM), BF16),
            pltpu.VMEM((heads, 2 * each, DIM), BF16),
            pltpu.VMEM((heads, 2 * each, DIM), BF16),
            pltpu.VMEM((heads, 2 * each, DIM), BF16),
            pltpu.VMEM((heads, 2 * each, DIM), BF16),
            dma((5,)),
            dma((2,)),
            dma((2,)),
            dma((2, 2)),
            dma((2, 2)),
            dma((2,)),
            dma((heads,)),
            dma((heads,)),
            dma((heads,)),
            dma((heads,)),
            pltpu.SemaphoreType.REGULAR,
        ],
        compiler_params=pltpu.CompilerParams(
            collective_id=0, has_side_effects=True, vmem_limit_bytes=40 * 1024 * 1024
        ),
    )(
        span_ids,
        flat(queries),
        flat(out_grad),
        flat(outputs),
        keys,
        values,
        log_norm,
    )
    return dq.reshape(queries.shape), dk, dv


def solution(mesh):
    in_specs = (
        P("ctx", "head", None),
        P("ctx", None),
        P("ctx", None),
        P("ctx", "head", None),
        P("ctx", "head", None),
        P("head", "ctx"),
        P(),
    )
    out_specs = (P("ctx", "head", None), P(("ctx", "head"), None), P(("ctx", "head"), None))
    return jax.shard_map(local, mesh=mesh, in_specs=in_specs, out_specs=out_specs, check_vma=False)
```

time: 253 us -> 45.8 us (0.18)
  waiting for transfers between devices: 164 us -> 0 us
  starting transfers between devices: 38.7 us -> 0 us
  Pallas kernels: 0 us -> 37.5 us
  matrix products: 25.8 us -> 0 us
  between operations: 14.6 us -> 0.66 us
  other arithmetic: 7.19 us -> 0 us
  local copies, waits for them, and re-layouts: 1.76 us -> 7.36 us
    reduce_scatter x2 -> x0, waiting for transfers between devices: 149 us -> none  [the longest x1 88.9 us: local(): lax.psum_scatter(value_acc, 'head', scatter_dimension=0, tiled=True)]
    ppermute x10 -> x0, starting transfers between devices: 38.6 us -> none  [shifted(): return lax.ppermute(block, axis, route)]
    pallas_call x0 -> x1, Pallas kernels: none -> 37.5 us  [local(): pl.pallas_call(body, out_shape=[jax.ShapeDtypeStruct((TOK, DIM), BF16), j...]
    dot_general x30 -> x0, matrix products: 25.8 us -> none  [the longest x6 6.93 us: tile_grads(): jnp.einsum('hqk,kd->qhd', dscore, key_rows, preferred_element_type=jnp.fl...]
    ppermute x10 -> x0, waiting for transfers between devices: 15 us -> none  [shifted(): return lax.ppermute(block, axis, route)]
    unnamed x33 -> x17, local copies, waits for them, and re-layouts: 1.05 us -> 7.36 us
    convert_element_type x3 -> x0, other arithmetic: 3.7 us -> none  [the longest x1 1.46 us: local(): key_sum.astype(jnp.bfloat16)]
  transfers between devices with their start and end apart: 12 -> 0, of which waited for: 6 -> 0; matrix products, arithmetic and copies ran while one was open for 13% -> 0% of each run, Pallas kernels for 0% -> 0%
where the time goes in v1:
time: 45.8 us; the launch traced here: 45.5 us
  Pallas kernels  37.5 us (82%)
  local copies, waits for them, and re-layouts  7.36 us (16%)
  between operations  0.66 us (1%)
    pallas_call x1, Pallas kernels, local(): pl.pallas_call(body, out_shape=[jax.ShapeDtypeStruct((TOK, DIM), BF16), j...  37.5 us
    unnamed x17, local copies, waits for them, and re-layouts  7.36 us

profile of v1, /device:TPU:1, one launch (start us, length us, event | category | flops | bytes accessed | tf_op | source)
XLA Modules:
  0.0 45.5 jit_solution(77630552547224120)
XLA Ops:
  0.6 0.0 copy-start.5
  0.6 0.0 copy-start.6
  0.7 0.7 %copy-done.5 = f32[1,1024]{1,0:T(1,128)S(1)} copy-done((f32[1,1024]{1,0:T(1,128)S(1)}, f32[1,1024]{1,0:T(1,128)}, u32[]{:S(2)}) %copy-start.5) | copy-done | bytes 4120
  1.3 0.0 copy-done.6
  1.3 0.0 copy-start
  1.3 0.9 %copy-done = bf16[1024,1,128]{2,0,1:T(8,128)(2,1)S(1)} copy-done((bf16[1024,1,128]{2,0,1:T(8,128)(2,1)S(1)}, bf16[1024,1,128]{2,0,1:T(8,128)(2,1)}, u32[]{:S(2)}) %copy-start) | copy-done | bytes 262168
  2.3 0.0 copy-start.1
  2.3 0.9 %copy-done.1 = bf16[1024,1,128]{2,0,1:T(8,128)(2,1)S(1)} copy-done((bf16[1024,1,128]{2,0,1:T(8,128)(2,1)S(1)}, bf16[1024,1,128]{2,0,1:T(8,128)(2,1)}, u32[]{:S(2)}) %copy-start.1) | copy-done | bytes 262168
  3.2 0.0 copy-start.2
  3.2 0.9 %copy-done.2 = bf16[1024,1,128]{2,0,1:T(8,128)(2,1)S(1)} copy-done((bf16[1024,1,128]{2,0,1:T(8,128)(2,1)S(1)}, bf16[1024,1,128]{2,0,1:T(8,128)(2,1)}, u32[]{:S(2)}) %copy-start.2) | copy-done | bytes 262168
  4.2 0.0 copy-start.3
  4.2 0.9 %copy-done.3 = bf16[1024,128]{1,0:T(8,128)(2,1)S(1)} copy-done((bf16[1024,128]{1,0:T(8,128)(2,1)S(1)}, bf16[1024,128]{1,0:T(8,128)(2,1)}, u32[]{:S(2)}) %copy-start.3) | copy-done | bytes 262168
  5.1 0.0 copy-start.4
  5.1 0.9 %copy-done.4 = bf16[1024,128]{1,0:T(8,128)(2,1)S(1)} copy-done((bf16[1024,128]{1,0:T(8,128)(2,1)S(1)}, bf16[1024,128]{1,0:T(8,128)(2,1)}, u32[]{:S(2)}) %copy-start.4) | copy-done | bytes 262168
  6.1 37.5 %shard_map.94 = (bf16[1024,128]{1,0:T(8,128)(2,1)S(1)}, bf16[128,128]{1,0:T(8,128)(2,1)S(1)}, bf16[128,128]{1,0:T(8,128)(2,1)S(1)}) custom-call(s32[128]{0:T(128)S(1)} %copy-done.6, bf16[1024,128]{1,0:T(8,128)(2,1)S(1)} %bitcast.4, bf16[1024,128]{1,0:T(8,128)(2,1)S(1)} %bitcast.5, bf16[1024,128]{1,0:T(8,128)(2,1)S(1)} %bitcast.6, ...), custom_call_target="tpu_custom_call" | custom-call | tf_op jit(solution)/shard_map/pallas_call | solution.py:323
  43.6 0.7 %copy.13 = bf16[1024,1,128]{2,0,1:T(8,128)(2,1)} copy(bf16[1024,1,128]{2,0,1:T(8,128)(2,1)S(1)} %bitcast.7) | data formatting | bytes 524288
  44.3 0.6 %copy.14 = bf16[128,128]{1,0:T(8,128)(2,1)} copy(bf16[128,128]{1,0:T(8,128)(2,1)S(1)} %get-tuple-element.13) | data formatting | bytes 65536
  44.9 0.6 %copy.15 = bf16[128,128]{1,0:T(8,128)(2,1)} copy(bf16[128,128]{1,0:T(8,128)(2,1)S(1)} %get-tuple-element.14) | data formatting | bytes 65536
Async XLA Ops:
  0.6 0.7 %copy-start.5 = (f32[1,1024]{1,0:T(1,128)S(1)}, f32[1,1024]{1,0:T(1,128)}, u32[]{:S(2)}) copy-start(f32[1,1024]{1,0:T(1,128)} %refs_6_.1) | copy-start | bytes 12292
  0.6 0.7 %copy-start.6 = (s32[128]{0:T(128)S(1)}, s32[128]{0:T(128)}, u32[]{:S(2)}) copy-start(s32[128]{0:T(128)} %refs_0_.1) | copy-start | bytes 1540
  1.3 1.0 %copy-start = (bf16[1024,1,128]{2,0,1:T(8,128)(2,1)S(1)}, bf16[1024,1,128]{2,0,1:T(8,128)(2,1)}, u32[]{:S(2)}) copy-start(bf16[1024,1,128]{2,0,1:T(8,128)(2,1)} %param.7) | copy-start | bytes 786436
  2.3 0.9 %copy-start.1 = (bf16[1024,1,128]{2,0,1:T(8,128)(2,1)S(1)}, bf16[1024,1,128]{2,0,1:T(8,128)(2,1)}, u32[]{:S(2)}) copy-start(bf16[1024,1,128]{2,0,1:T(8,128)(2,1)} %param.11) | copy-start | bytes 786436
  3.2 0.9 %copy-start.2 = (bf16[1024,1,128]{2,0,1:T(8,128)(2,1)S(1)}, bf16[1024,1,128]{2,0,1:T(8,128)(2,1)}, u32[]{:S(2)}) copy-start(bf16[1024,1,128]{2,0,1:T(8,128)(2,1)} %param.10) | copy-start | bytes 786436
  4.2 0.9 %copy-start.3 = (bf16[1024,128]{1,0:T(8,128)(2,1)S(1)}, bf16[1024,128]{1,0:T(8,128)(2,1)}, u32[]{:S(2)}) copy-start(bf16[1024,128]{1,0:T(8,128)(2,1)} %refs_4_.1) | copy-start | bytes 786436
  5.1 0.9 %copy-start.4 = (bf16[1024,128]{1,0:T(8,128)(2,1)S(1)}, bf16[1024,128]{1,0:T(8,128)(2,1)}, u32[]{:S(2)}) copy-start(bf16[1024,128]{1,0:T(8,128)(2,1)} %refs_5_.1) | copy-start | bytes 786436

commit v2 on v1

--- a/solution.py
+++ b/solution.py
@@ -12,6 +12,8 @@
 NT = (((1,), (1,)), ((), ()))
 TN = (((0,), (0,)), ((), ()))
 SPAN = 512
+LINE = 16
+VMEM_GRANT = 63 * 1024 * 1024
 TOK = 2 * SPAN
 DIM = 128
 SCALE = DIM ** -0.5
@@ -32,8 +34,8 @@
 
 
 def kernel(
-    holders, heads, span_ref, q_in, g_in, o_in, k_in, v_in, norm_in, dq_out, dk_out, dv_out,
-    raw_q, raw_g, raw_k, raw_v, raw_o, q_own, q_far, kv_own, kv_mate, kv_far,
+    holders, heads, span_in, q_in, g_in, o_in, k_in, v_in, norm_in, dq_out, dk_out, dv_out,
+    span_ref, raw_norm, raw_q, raw_g, raw_k, raw_v, raw_o, q_own, q_far, kv_own, kv_mate, kv_far,
     norm_own, norm_far, delta_own, delta_far, dq_acc, dk_acc, dv_acc, dq_end, dk_end, dv_end,
     mate_out, mate_part, next_out, dq_part, back_out, back_part, own_out, own_part,
     load_sem, kv_sem, mate_sem, far_sem, row_sem, dq_sem, back_send, back_recv, own_send, own_recv, ready,
@@ -46,10 +48,16 @@
     ahead = lax.rem(c + 2, holders)
     behind = lax.rem(c + holders - 2, holders)
 
+    place_in_line = lax.rem(lax.div(c, 2), LINE)
+    start_of_line, last = place_in_line == 0, place_in_line == LINE - 1
+
     loads = [
         pltpu.make_async_copy(ref, raw, load_sem.at[i])
         for i, (ref, raw) in enumerate(
-            ((q_in, raw_q), (g_in, raw_g), (k_in, raw_k), (v_in, raw_v), (o_in, raw_o))
+            (
+                (span_in, span_ref), (k_in, raw_k), (v_in, raw_v), (q_in, raw_q), (g_in, raw_g),
+                (norm_in, raw_norm), (o_in, raw_o),
+            )
         )
     ]
     for copy in loads:
@@ -58,10 +66,17 @@
     barrier = pltpu.get_barrier_semaphore()
     pl.semaphore_signal(barrier, inc=1, device_id=mate, device_id_type=MESH)
     pl.semaphore_signal(barrier, inc=1, device_id={"ctx": behind}, device_id_type=MESH)
+
+    @pl.when(jnp.logical_not(last))
+    def _():
+        pl.semaphore_signal(barrier, inc=1, device_id={"ctx": ahead}, device_id_type=MESH)
+
     for step in range(1, heads):
         pl.semaphore_signal(
             barrier, inc=1, device_id={"head": lax.rem(h + step, heads)}, device_id_type=MESH
         )
+
+    loads[0].wait()
 
     def first(holder):
         return span_ref[2 * holder]
@@ -83,19 +98,25 @@
     ]
 
     lo, hi = low_place * SPAN, (1 - low_place) * SPAN
-    for copy in loads[:4]:
+    for copy in loads[1:5]:
         copy.wait()
     for i, (raw, place) in enumerate(((raw_q, hi), (raw_g, hi), (raw_q, lo), (raw_g, lo))):
         q_own[pl.ds(i * SPAN, SPAN)] = raw[pl.ds(place, SPAN)]
     for i, (raw, place) in enumerate(((raw_k, lo), (raw_v, lo), (raw_k, hi), (raw_v, hi))):
         kv_own[pl.ds(i * SPAN, SPAN)] = raw[pl.ds(place, SPAN)]
-    loads[4].wait()
+    for copy in loads[5:]:
+        copy.wait()
     for i, place in enumerate((hi, lo)):
-        norm_own[:, pl.ds(i * SPAN, SPAN)] = norm_in[:, pl.ds(place, SPAN)] * LOG2E
+        norm_own[:, pl.ds(i * SPAN, SPAN)] = raw_norm[:, pl.ds(place, SPAN)] * LOG2E
         product = raw_g[pl.ds(place, SPAN)].astype(F32) * raw_o[pl.ds(place, SPAN)].astype(F32)
         delta_own[:, pl.ds(i * SPAN, SPAN)] = jnp.sum(product.T, axis=0, keepdims=True)
 
-    pl.semaphore_wait(barrier, heads + 1)
+    pl.semaphore_wait(barrier, jnp.where(start_of_line, heads + 1, heads + 2))
+
+    @pl.when(last)
+    def _():
+        pl.semaphore_signal(ready, inc=1, device_id={"ctx": ahead}, device_id_type=MESH)
+
 
     def remote(src, dst, send, recv, device):
         return pltpu.make_async_remote_copy(
@@ -124,12 +145,11 @@
         for copy in back_copies:
             copy.start()
 
-    @pl.when(even)
-    def _():
-        pl.semaphore_signal(ready, inc=1, device_id={"ctx": ahead}, device_id_type=MESH)
-        pl.semaphore_wait(ready, 1)
+    def send_queries():
         for copy in (*row_copies, *q_copies):
             copy.start()
+
+    pl.when(jnp.logical_and(even, jnp.logical_not(start_of_line)))(send_queries)
 
     def either(a, b):
         return a + b - 2 * a * b
@@ -173,6 +193,12 @@
     dq_acc[0, pl.ds(0, SPAN)] += dq
     dk_acc[0, pl.ds(SPAN, SPAN)] = dk
     dv_acc[0, pl.ds(SPAN, SPAN)] = dv
+
+    @pl.when(start_of_line)
+    def _():
+        pl.semaphore_wait(ready, 1)
+
+    pl.when(jnp.logical_and(even, start_of_line))(send_queries)
 
     for ref in (dk_acc, dv_acc):
         for slot in (1, 2):
@@ -224,12 +250,7 @@
 
     low_of = [low_place, 1 - low_place]
 
-    @pl.when(odd)
-    def _():
-        kv_copy.wait_recv()
-        crossing(0, 1, False, True)
-        level(0, 0, 1)
-        send_mate()
+    def visit_behind():
         back_copies[0].wait_recv()
         crossing(0, 2, False, True)
         back_copies[1].wait_recv()
@@ -245,6 +266,15 @@
                     back_out[p * (heads // 2) + s, pl.ds(i * each, each)] = value[s * each : (s + 1) * each]
         for copy in back_sends:
             copy.start()
+
+    @pl.when(odd)
+    def _():
+        kv_copy.wait_recv()
+        crossing(0, 1, False, True)
+        level(0, 0, 1)
+        send_mate()
+
+    pl.when(jnp.logical_and(odd, jnp.logical_not(start_of_line)))(visit_behind)
 
     mate_copy.wait_recv()
     each = TOK // heads
@@ -263,6 +293,8 @@
         own_sends[-1].start()
     own_part[h] = own_out[h]
 
+    pl.when(jnp.logical_and(odd, start_of_line))(visit_behind)
+
     @pl.when(even)
     def _():
         dq_copy.wait_recv()
@@ -312,6 +344,17 @@
     def _():
         for copy in (*back_copies, *back_sends):
             copy.wait_send()
+
+
+def store(dq, dk, dv, dq_out, dk_out, dv_out, sem):
+    copies = [
+        pltpu.make_async_copy(src, dst, sem.at[i])
+        for i, (src, dst) in enumerate(((dq, dq_out), (dk, dk_out), (dv, dv_out)))
+    ]
+    for copy in copies:
+        copy.start()
+    for copy in copies:
+        copy.wait()
 
 
 def local(queries, keys, values, outputs, out_grad, log_norm, span_ids):
@@ -328,12 +371,12 @@
             jax.ShapeDtypeStruct((each, DIM), BF16),
         ],
         in_specs=[
-            pl.BlockSpec(memory_space=pltpu.SMEM),
-            *[pl.BlockSpec(memory_space=pl.ANY)] * 5,
-            pl.BlockSpec(memory_space=pltpu.VMEM),
+            *[pl.BlockSpec(memory_space=pltpu.HBM)] * 7,
         ],
         out_specs=[pl.BlockSpec(memory_space=pltpu.VMEM)] * 3,
         scratch_shapes=[
+            pltpu.SMEM((2 * holders,), jnp.int32),
+            pltpu.VMEM((1, TOK), F32),
             *[pltpu.VMEM((TOK, DIM), BF16)] * 5,
             *[pltpu.VMEM((2 * TOK, DIM), BF16)] * 5,
             *[pltpu.VMEM((1, TOK), F32)] * 4,
@@ -351,7 +394,7 @@
             pltpu.VMEM((heads, 2 * each, DIM), BF16),
             pltpu.VMEM((heads, 2 * each, DIM), BF16),
             pltpu.VMEM((heads, 2 * each, DIM), BF16),
-            dma((5,)),
+            dma((7,)),
             dma((2,)),
             dma((2,)),
             dma((2, 2)),
@@ -364,7 +407,7 @@
             pltpu.SemaphoreType.REGULAR,
         ],
         compiler_params=pltpu.CompilerParams(
-            collective_id=0, has_side_effects=True, vmem_limit_bytes=40 * 1024 * 1024
+            collective_id=0, has_side_effects=True, vmem_limit_bytes=VMEM_GRANT
         ),
     )(
         span_ids,
@@ -375,6 +418,13 @@
         values,
         log_norm,
     )
+    dq, dk, dv = pl.pallas_call(
+        store,
+        out_shape=[jax.ShapeDtypeStruct(a.shape, BF16) for a in (dq, dk, dv)],
+        in_specs=[pl.BlockSpec(memory_space=pltpu.VMEM)] * 3,
+        out_specs=[pl.BlockSpec(memory_space=pltpu.HBM)] * 3,
+        scratch_shapes=[dma((3,))],
+    )(dq, dk, dv)
     return dq.reshape(queries.shape), dk, dv
 
 

time: 45.8 us -> 37.5 us (0.82)
  the two profiles are of different devices: /device:TPU:1 before, /device:TPU:8 now
where the time goes in v2:
time: 37.5 us; the launch traced here: 37.4 us
  Pallas kernels  36.7 us (98%)
  between operations  0.64 us (2%)
    pallas_call x1, Pallas kernels, local(): pl.pallas_call(body, out_shape=[jax.ShapeDtypeStruct((TOK, DIM), BF16), j...  35 us
    pallas_call x1, Pallas kernels, local(): pl.pallas_call(store, out_shape=[jax.ShapeDtypeStruct(a.shape, BF16) for...  1.71 us

profile of v2, /device:TPU:8, one launch (start us, length us, event | category | flops | bytes accessed | tf_op | source)
XLA Modules:
  0.0 37.4 jit_solution(7452882807899626587)
XLA Ops:
  0.6 35.0 %shard_map.94 = (bf16[1024,128]{1,0:T(8,128)(2,1)}, bf16[128,128]{1,0:T(8,128)(2,1)}, bf16[128,128]{1,0:T(8,128)(2,1)}) custom-call(s32[128]{0:T(128)} %refs_0_.1, bf16[1024,128]{1,0:T(8,128)(2,1)} %bitcast.4, bf16[1024,128]{1,0:T(8,128)(2,1)} %bitcast.5, bf16[1024,128]{1,0:T(8,128)(2,1)} %bitcast.6, bf16[1024,128]{1,0:T(8,128)(2,1)} %refs_4_.1, ...), custom_call_target="tpu_custom_call" | custom-call | tf_op jit(solution)/shard_map/pallas_call | solution.py:366
  35.6 1.7 %shard_map.95 = (bf16[1024,128]{1,0:T(8,128)(2,1)}, bf16[128,128]{1,0:T(8,128)(2,1)}, bf16[128,128]{1,0:T(8,128)(2,1)}) custom-call(bf16[1024,128]{1,0:T(8,128)(2,1)} %get-tuple-element.9.dq, bf16[128,128]{1,0:T(8,128)(2,1)} %get-tuple-element.10.dk, bf16[128,128]{1,0:T(8,128)(2,1)} %get-tuple-element.11.dv), custom_call_target="tpu_custom_call" | custom-call | tf_op jit(solution)/shard_map/pallas_call | solution.py:421

commit v3 on v2

--- a/solution.py
+++ b/solution.py
@@ -38,7 +38,7 @@
     span_ref, raw_norm, raw_q, raw_g, raw_k, raw_v, raw_o, q_own, q_far, kv_own, kv_mate, kv_far,
     norm_own, norm_far, delta_own, delta_far, dq_acc, dk_acc, dv_acc, dq_end, dk_end, dv_end,
     mate_out, mate_part, next_out, dq_part, back_out, back_part, own_out, own_part,
-    load_sem, kv_sem, mate_sem, far_sem, row_sem, dq_sem, back_send, back_recv, own_send, own_recv, ready,
+    load_sem, kv_sem, mate_sem, far_sem, row_sem, dq_sem, back_send, back_recv, own_send, own_recv, hello, relay, plane,
 ):
     c = lax.axis_index("ctx")
     h = lax.axis_index("head")
@@ -49,7 +49,9 @@
     behind = lax.rem(c + holders - 2, holders)
 
     place_in_line = lax.rem(lax.div(c, 2), LINE)
-    start_of_line, last = place_in_line == 0, place_in_line == LINE - 1
+    start_of_line, end_of_line = place_in_line == 0, place_in_line == LINE - 1
+    is_odd_place = lax.rem(place_in_line, 2) == 1
+    is_even_place = lax.rem(place_in_line, 2) == 0
 
     loads = [
         pltpu.make_async_copy(ref, raw, load_sem.at[i])
@@ -64,17 +66,37 @@
         copy.start()
 
     barrier = pltpu.get_barrier_semaphore()
-    pl.semaphore_signal(barrier, inc=1, device_id=mate, device_id_type=MESH)
-    pl.semaphore_signal(barrier, inc=1, device_id={"ctx": behind}, device_id_type=MESH)
-
-    @pl.when(jnp.logical_not(last))
-    def _():
-        pl.semaphore_signal(barrier, inc=1, device_id={"ctx": ahead}, device_id_type=MESH)
-
-    for step in range(1, heads):
-        pl.semaphore_signal(
-            barrier, inc=1, device_id={"head": lax.rem(h + step, heads)}, device_id_type=MESH
-        )
+
+    def tell(sem, **device):
+        pl.semaphore_signal(sem, inc=1, device_id=device, device_id_type=MESH)
+
+    def tell_heads(sem):
+        for step in range(1, heads):
+            tell(sem, head=lax.rem(h + step, heads))
+
+    @pl.when(is_even_place)
+    def _():
+        for holder in (ahead, behind):
+            tell(barrier, ctx=holder)
+            tell(barrier, ctx=holder + 1 - 2 * side)
+        tell_heads(barrier)
+
+    wants_behind = jnp.logical_and(even, jnp.logical_not(start_of_line))
+
+    @pl.when(jnp.logical_and(is_even_place, wants_behind))
+    def _():
+        pl.semaphore_wait(hello.at[1], 1)
+
+    @pl.when(jnp.logical_and(is_even_place, jnp.logical_not(wants_behind)))
+    def _():
+        pl.semaphore_wait(hello.at[0], 1)
+
+    @pl.when(is_odd_place)
+    def _():
+        tell(barrier, **mate)
+        pl.semaphore_wait(barrier, 5)
+        tell(hello.at[0], ctx=behind)
+        tell(hello.at[1], ctx=ahead)
 
     loads[0].wait()
 
@@ -104,20 +126,6 @@
         q_own[pl.ds(i * SPAN, SPAN)] = raw[pl.ds(place, SPAN)]
     for i, (raw, place) in enumerate(((raw_k, lo), (raw_v, lo), (raw_k, hi), (raw_v, hi))):
         kv_own[pl.ds(i * SPAN, SPAN)] = raw[pl.ds(place, SPAN)]
-    for copy in loads[5:]:
-        copy.wait()
-    for i, place in enumerate((hi, lo)):
-        norm_own[:, pl.ds(i * SPAN, SPAN)] = raw_norm[:, pl.ds(place, SPAN)] * LOG2E
-        product = raw_g[pl.ds(place, SPAN)].astype(F32) * raw_o[pl.ds(place, SPAN)].astype(F32)
-        delta_own[:, pl.ds(i * SPAN, SPAN)] = jnp.sum(product.T, axis=0, keepdims=True)
-
-    pl.semaphore_wait(barrier, jnp.where(start_of_line, heads + 1, heads + 2))
-
-    @pl.when(last)
-    def _():
-        pl.semaphore_signal(ready, inc=1, device_id={"ctx": ahead}, device_id_type=MESH)
-
-
     def remote(src, dst, send, recv, device):
         return pltpu.make_async_remote_copy(
             src_ref=src, dst_ref=dst, send_sem=send, recv_sem=recv, device_id=device, device_id_type=MESH
@@ -138,18 +146,28 @@
         for i in range(2)
     ]
 
+    @pl.when(odd)
+    def _():
+        back_copies[0].start()
+
+    def send_queries():
+        q_copies[0].start()
+
+    pl.when(jnp.logical_and(even, jnp.logical_not(start_of_line)))(send_queries)
     kv_copy.start()
 
-    @pl.when(odd)
-    def _():
-        for copy in back_copies:
+    for copy in loads[5:]:
+        copy.wait()
+    for i, place in enumerate((hi, lo)):
+        norm_own[:, pl.ds(i * SPAN, SPAN)] = raw_norm[:, pl.ds(place, SPAN)] * LOG2E
+        product = raw_g[pl.ds(place, SPAN)].astype(F32) * raw_o[pl.ds(place, SPAN)].astype(F32)
+        delta_own[:, pl.ds(i * SPAN, SPAN)] = jnp.sum(product.T, axis=0, keepdims=True)
+
+    def send_rows():
+        for copy in row_copies:
             copy.start()
 
-    def send_queries():
-        for copy in (*row_copies, *q_copies):
-            copy.start()
-
-    pl.when(jnp.logical_and(even, jnp.logical_not(start_of_line)))(send_queries)
+    pl.when(jnp.logical_and(even, jnp.logical_not(start_of_line)))(send_rows)
 
     def either(a, b):
         return a + b - 2 * a * b
@@ -194,15 +212,34 @@
     dk_acc[0, pl.ds(SPAN, SPAN)] = dk
     dv_acc[0, pl.ds(SPAN, SPAN)] = dv
 
-    @pl.when(start_of_line)
-    def _():
-        pl.semaphore_wait(ready, 1)
+    @pl.when(odd)
+    def _():
+        back_copies[1].start()
+
+    pl.when(jnp.logical_and(even, jnp.logical_not(start_of_line)))(q_copies[1].start)
+
+    @pl.when(jnp.logical_and(is_even_place, wants_behind))
+    def _():
+        pl.semaphore_wait(hello.at[0], 1)
+
+    @pl.when(is_even_place)
+    def _():
+        pl.semaphore_wait(barrier, heads - 1)
+        tell_heads(relay)
+
+    @pl.when(jnp.logical_and(even, start_of_line))
+    def _():
+        pl.semaphore_wait(hello.at[1], 1)
 
     pl.when(jnp.logical_and(even, start_of_line))(send_queries)
-
-    for ref in (dk_acc, dv_acc):
-        for slot in (1, 2):
-            ref[slot, pl.ds(SPAN, SPAN)] = jnp.zeros((SPAN, DIM), F32)
+    pl.when(jnp.logical_and(even, start_of_line))(send_rows)
+
+    def tell_ahead():
+        @pl.when(is_even_place)
+        def _():
+            pl.semaphore_wait(relay, heads - 1)
+            tell(plane, ctx=ahead)
+
     for ref in (dq_end, dk_end, dv_end):
         for pair in range(2):
             ref[pair, pl.ds(SPAN, SPAN)] = jnp.zeros((SPAN, DIM), F32)
@@ -222,24 +259,34 @@
         mate_copy.start()
 
     dq_copy = remote(next_out, dq_part, dq_sem.at[0], dq_sem.at[1], {"ctx": ahead})
-    back_sends = [
-        remote(
-            back_out.at[to], back_part.at[h], back_send.at[to], back_recv.at[h], {"ctx": behind, "head": to}
-        )
-        for to in range(heads)
-    ]
+    chunks = heads // 2
+    each = TOK // heads
+    order = [lax.rem(h + step, chunks) for step in range(1, chunks + 1)]
+
+    def chunk_copy(i):
+        return remote(back_out.at[i], back_part.at[i], back_send.at[i], back_recv.at[i], {"ctx": behind})
+
+    def send_back(block, dk, dv):
+        for r in range(chunks):
+            rows = slice(r * each, (r + 1) * each)
+            back_out[block * chunks + r, pl.ds(0, each)] = (dk[rows] * SCALE).astype(BF16)
+            back_out[block * chunks + r, pl.ds(each, each)] = dv[rows].astype(BF16)
+        for r in order:
+            chunk_copy(block * chunks + r).start()
 
     @pl.when(even)
     def _():
         kv_copy.wait_recv()
         for copy in row_copies:
             copy.wait_recv()
+        tell_ahead()
         q_copies[0].wait_recv()
         crossing(1, 1, True, True)
         crossing(1, 0, False, False)
+        pl.when(start_of_line)(q_copies[1].start)
         q_copies[1].wait_recv()
         level(0, 1, 1)
-        send_mate()
+        pl.when(jnp.logical_not(end_of_line))(send_mate)
         level(1, 1, 0)
         for part in range(2):
             value = if_low(0, 1 - part, dq_end) + if_low(1, 1 - part, dq_end)
@@ -247,25 +294,23 @@
                 value += dq_acc[1, pl.ds(0, SPAN)]
             next_out[pl.ds(part * SPAN, SPAN)] = (value * SCALE).astype(BF16)
         dq_copy.start()
+        pl.when(end_of_line)(send_mate)
 
     low_of = [low_place, 1 - low_place]
 
     def visit_behind():
+        @pl.when(is_even_place)
+        def _():
+            pl.semaphore_wait(hello.at[1], 1)
+
         back_copies[0].wait_recv()
-        crossing(0, 2, False, True)
+        dq, dk, dv = block(0, 0, 2, 0)
+        dq_acc[0, pl.ds(0, SPAN)] += dq
+        send_back(0, dk, dv)
         back_copies[1].wait_recv()
-        level(1, 0, 2)
-        place = late(behind)
-        for p in range(2):
-            part = either(place, p)
-            for i, (acc, end, factor) in enumerate(((dk_acc, dk_end, SCALE), (dv_acc, dv_end, 1.0))):
-                value = if_low(1, part, end) + acc[2, at(part, SPAN)]
-                value = (value * factor).astype(BF16)
-                each = TOK // heads
-                for s in range(heads // 2):
-                    back_out[p * (heads // 2) + s, pl.ds(i * each, each)] = value[s * each : (s + 1) * each]
-        for copy in back_sends:
-            copy.start()
+        dq, dk, dv = block(0, lows[1], 2, 1 - lows[1])
+        dq_end[1, pl.ds(0, SPAN)] = dq
+        send_back(1, dk, dv)
 
     @pl.when(odd)
     def _():
@@ -273,35 +318,70 @@
         crossing(0, 1, False, True)
         level(0, 0, 1)
         send_mate()
-
-    pl.when(jnp.logical_and(odd, jnp.logical_not(start_of_line)))(visit_behind)
+        tell_ahead()
+
+    pl.when(odd)(visit_behind)
 
     mate_copy.wait_recv()
-    each = TOK // heads
-    for p in range(2):
-        part = low_of[p]
-        for i, (acc, end, factor) in enumerate(((dk_acc, dk_end, SCALE), (dv_acc, dv_end, 1.0))):
-            value = (acc[0, at(part, SPAN)] + if_low(1, part, end, 1 - side)) * factor
-            value += mate_part[at(2 * part + i, SPAN)].astype(F32)
-            value = value.astype(BF16)
-            for s in range(heads // 2):
-                own_out[p * (heads // 2) + s, pl.ds(i * each, each)] = value[s * each : (s + 1) * each]
-    own_sends = []
-    for step in range(1, heads):
-        to = lax.rem(h + step, heads)
-        own_sends.append(remote(own_out.at[to], own_part.at[h], own_send.at[to], own_recv.at[h], {"head": to}))
-        own_sends[-1].start()
+
+    @pl.when(is_odd_place)
+    def _():
+        pl.semaphore_wait(plane, 1)
+
+    def own_copy(to):
+        return remote(own_out.at[to], own_part.at[h], own_send.at[to], own_recv.at[h], {"head": to})
+
+    next_low = (low_span(c) < low_span(ahead)).astype(jnp.int32)
+    for step, r in enumerate(order):
+
+        @pl.when(odd)
+        def _():
+            chunk_copy(r).wait_recv()
+            chunk_copy(chunks + r).wait_recv()
+
+        for p in range(2):
+            part = low_of[p]
+            to = p * chunks + r
+            row = r * each
+
+            def rows_of(i):
+                return pl.ds(i * SPAN + row, each)
+
+            halves = []
+            for i, (acc, end, factor) in enumerate(((dk_acc, dk_end, SCALE), (dv_acc, dv_end, 1.0))):
+                add = end[1, rows_of(1 - (1 - side) * either(lows[1], part))]
+                value = (acc[0, rows_of(part)] + add) * factor
+                halves.append(value + mate_part[rows_of(2 * part + i)].astype(F32))
+
+            @pl.when(even)
+            def _():
+                for i in range(2):
+                    own_out[to, pl.ds(i * each, each)] = halves[i].astype(BF16)
+
+            @pl.when(odd)
+            def _():
+                for i in range(2):
+                    value = halves[i]
+                    for place, on in ((r, 1 - part), (chunks + r, either(next_low, part))):
+                        there = jnp.full((each, DIM), on, jnp.int32) == 1
+                        back = back_part[place, pl.ds(i * each, each)].astype(F32)
+                        value += jnp.where(there, back, 0.0)
+                    own_out[to, pl.ds(i * each, each)] = value.astype(BF16)
+
+            if step < chunks - 1:
+                own_copy(to).start()
+            else:
+                pl.when(to != h)(own_copy(to).start)
     own_part[h] = own_out[h]
 
-    pl.when(jnp.logical_and(odd, start_of_line))(visit_behind)
-
-    @pl.when(even)
-    def _():
+    def finish_queries():
         dq_copy.wait_recv()
         for p in range(2):
             place = (1 - low_of[p]) * SPAN
             value = dq_acc[0, pl.ds(place, SPAN)] * SCALE + dq_part[pl.ds(place, SPAN)].astype(F32)
             dq_out[pl.ds(p * SPAN, SPAN)] = value.astype(BF16)
+
+    pl.when(wants_behind)(finish_queries)
 
     @pl.when(odd)
     def _():
@@ -319,21 +399,12 @@
         total += own_part[i].astype(F32)
     dk_out[...] = total[:each].astype(BF16)
     dv_out[...] = total[each:].astype(BF16)
-
-    @pl.when(odd)
-    def _():
-        for i in range(heads):
-            remote(back_out.at[i], back_part.at[i], back_send.at[i], back_recv.at[i], mate).wait_recv()
-        more = total
-        for i in range(heads):
-            more += back_part[i].astype(F32)
-        dk_out[...] = more[:each].astype(BF16)
-        dv_out[...] = more[each:].astype(BF16)
+    pl.when(jnp.logical_and(even, start_of_line))(finish_queries)
 
     kv_copy.wait_send()
     mate_copy.wait_send()
-    for copy in own_sends:
-        copy.wait_send()
+    for step in range(1, heads):
+        own_copy(lax.rem(h + step, heads)).wait_send()
 
     @pl.when(even)
     def _():
@@ -342,7 +413,7 @@
 
     @pl.when(odd)
     def _():
-        for copy in (*back_copies, *back_sends):
+        for copy in (*back_copies, *(chunk_copy(i) for i in range(heads))):
             copy.wait_send()
 
 
@@ -381,8 +452,8 @@
             *[pltpu.VMEM((2 * TOK, DIM), BF16)] * 5,
             *[pltpu.VMEM((1, TOK), F32)] * 4,
             pltpu.VMEM((2, TOK, DIM), F32),
-            pltpu.VMEM((3, TOK, DIM), F32),
-            pltpu.VMEM((3, TOK, DIM), F32),
+            pltpu.VMEM((2, TOK, DIM), F32),
+            pltpu.VMEM((2, TOK, DIM), F32),
             pltpu.VMEM((2, TOK, DIM), F32),
             pltpu.VMEM((2, TOK, DIM), F32),
             pltpu.VMEM((2, TOK, DIM), F32),
@@ -404,6 +475,8 @@
             dma((heads,)),
             dma((heads,)),
             dma((heads,)),
+            pltpu.SemaphoreType.REGULAR((2,)),
+            pltpu.SemaphoreType.REGULAR,
             pltpu.SemaphoreType.REGULAR,
         ],
         compiler_params=pltpu.CompilerParams(

time: 37.5 us -> 35.2 us (0.939)
  the two profiles are of different devices: /device:TPU:8 before, /device:TPU:6 now
where the time goes in v3:
time: 35.2 us; the launch traced here: 35 us
  Pallas kernels  34.4 us (98%)
  between operations  0.64 us (2%)
    pallas_call x1, Pallas kernels, local(): pl.pallas_call(body, out_shape=[jax.ShapeDtypeStruct((TOK, DIM), BF16), j...  32.7 us
    pallas_call x1, Pallas kernels, local(): pl.pallas_call(store, out_shape=[jax.ShapeDtypeStruct(a.shape, BF16) for...  1.71 us

profile of v3, /device:TPU:6, one launch (start us, length us, event | category | flops | bytes accessed | tf_op | source)
XLA Modules:
  0.0 35.0 jit_solution(11537495571907280302)
XLA Ops:
  0.6 32.7 %shard_map.94 = (bf16[1024,128]{1,0:T(8,128)(2,1)}, bf16[128,128]{1,0:T(8,128)(2,1)}, bf16[128,128]{1,0:T(8,128)(2,1)}) custom-call(s32[128]{0:T(128)} %refs_0_.1, bf16[1024,128]{1,0:T(8,128)(2,1)} %bitcast.4, bf16[1024,128]{1,0:T(8,128)(2,1)} %bitcast.5, bf16[1024,128]{1,0:T(8,128)(2,1)} %bitcast.6, bf16[1024,128]{1,0:T(8,128)(2,1)} %refs_4_.1, ...), custom_call_target="tpu_custom_call" | custom-call | tf_op jit(solution)/shard_map/pallas_call | solution.py:437
  33.3 1.7 %shard_map.95 = (bf16[1024,128]{1,0:T(8,128)(2,1)}, bf16[128,128]{1,0:T(8,128)(2,1)}, bf16[128,128]{1,0:T(8,128)(2,1)}) custom-call(bf16[1024,128]{1,0:T(8,128)(2,1)} %get-tuple-element.9.dq, bf16[128,128]{1,0:T(8,128)(2,1)} %get-tuple-element.10.dk, bf16[128,128]{1,0:T(8,128)(2,1)} %get-tuple-element.11.dv), custom_call_target="tpu_custom_call" | custom-call | tf_op jit(solution)/shard_map/pallas_call | solution.py:494

commit v4 on v3

v4 whole, which is shorter than its diff:
```python
import jax
import jax.numpy as jnp
from jax import lax
from jax.experimental import pallas as pl
from jax.experimental.pallas import tpu as pltpu
from jax.sharding import PartitionSpec as P

MESH = pl.DeviceIdType.MESH
F32 = jnp.float32
BF16 = jnp.bfloat16
LOG2E = 1.4426950408889634
NT = (((1,), (1,)), ((), ()))
TN = (((0,), (0,)), ((), ()))
SPAN = 512
LINE = 16
VMEM_GRANT = 63 * 1024 * 1024
TOK = 2 * SPAN
DIM = 128
SCALE = DIM ** -0.5


def tile(q, g, norm, delta, k, v, diagonal=False):
    score = lax.dot_general(k, q, NT, preferred_element_type=F32)
    prob = jnp.exp2(score * (SCALE * LOG2E) - norm)
    if diagonal:
        rows = lax.broadcasted_iota(jnp.int32, score.shape, 0)
        prob = jnp.where(rows <= lax.broadcasted_iota(jnp.int32, score.shape, 1), prob, 0.0)
    dprob = lax.dot_general(v, g, NT, preferred_element_type=F32)
    dscore = (prob * (dprob - delta)).astype(BF16)
    dv = jnp.dot(prob.astype(BF16), g, preferred_element_type=F32)
    dk = jnp.dot(dscore, q, preferred_element_type=F32)
    dq = lax.dot_general(dscore, k, TN, preferred_element_type=F32)
    return dq, dk, dv


def kernel(
    holders, heads, span_in, q_in, g_in, o_in, k_in, v_in, norm_in, dq_out, dkv_out,
    span_ref, raw_norm, raw_q, raw_g, raw_k, raw_v, raw_o, q_own, kv_own, kv_mate,
    *rest,
):
    chunks = heads // 2
    q_far, kv_far, dq_part, back_part = (rest[i * chunks : (i + 1) * chunks] for i in range(4))
    (
        norm_own, norm_far, delta_own, delta_far, dq_acc, dk_acc, dv_acc, dq_end, dk_end, dv_end,
        mate_out, mate_part, next_out, back_out, own_out, own_part,
        load_sem, kv_sem, mate_sem, far_sem, row_sem, dq_sem, back_sem, own_send, own_recv,
        hello, relay, plane,
    ) = rest[4 * chunks :]
    each = TOK // heads
    c = lax.axis_index("ctx")
    h = lax.axis_index("head")
    side = lax.rem(c, 2)
    even, odd = side == 0, side == 1
    mate = {"ctx": c + 1 - 2 * side}
    ahead = lax.rem(c + 2, holders)
    behind = lax.rem(c + holders - 2, holders)

    place_in_line = lax.rem(lax.div(c, 2), LINE)
    start_of_line, end_of_line = place_in_line == 0, place_in_line == LINE - 1
    is_odd_place = lax.rem(place_in_line, 2) == 1
    is_even_place = lax.rem(place_in_line, 2) == 0

    loads = [
        pltpu.make_async_copy(ref, raw, load_sem.at[i])
        for i, (ref, raw) in enumerate(
            (
                (span_in, span_ref), (k_in, raw_k), (v_in, raw_v), (q_in, raw_q), (g_in, raw_g),
                (norm_in, raw_norm), (o_in, raw_o),
            )
        )
    ]
    for copy in loads:
        copy.start()

    barrier = pltpu.get_barrier_semaphore()

    def tell(sem, **device):
        pl.semaphore_signal(sem, inc=1, device_id=device, device_id_type=MESH)

    def tell_heads(sem):
        for step in range(1, heads):
            tell(sem, head=lax.rem(h + step, heads))

    @pl.when(is_even_place)
    def _():
        for holder in (ahead, behind):
            tell(barrier, ctx=holder)
            tell(barrier, ctx=holder + 1 - 2 * side)
        tell_heads(barrier)

    wants_behind = jnp.logical_and(even, jnp.logical_not(start_of_line))

    @pl.when(jnp.logical_and(is_even_place, wants_behind))
    def _():
        pl.semaphore_wait(hello.at[1], 1)

    @pl.when(jnp.logical_and(is_even_place, jnp.logical_not(wants_behind)))
    def _():
        pl.semaphore_wait(hello.at[0], 1)

    @pl.when(is_odd_place)
    def _():
        tell(barrier, **mate)
        pl.semaphore_wait(barrier, 5)
        tell(hello.at[0], ctx=behind)
        tell(hello.at[1], ctx=ahead)

    loads[0].wait()

    def first(holder):
        return span_ref[2 * holder]

    def second(holder):
        return span_ref[2 * holder + 1]

    def low_span(holder):
        return jnp.minimum(first(holder), second(holder))

    def late(holder):
        return (first(holder) > second(holder)).astype(jnp.int32)

    low_place = late(c)
    asks = jnp.where(even, ahead, c)
    lows = [
        (low_span(c + 1 - 2 * side) < low_span(asks)).astype(jnp.int32),
        (low_span(jnp.where(even, c, behind)) < low_span(asks)).astype(jnp.int32),
    ]

    lo, hi = low_place * SPAN, (1 - low_place) * SPAN

    def by_chunk(ref, i, value):
        for r in range(chunks):
            ref[r, pl.ds(i * each, each)] = value[r * each : (r + 1) * each]

    for copy in loads[1:5]:
        copy.wait()
    for i, (raw, place) in enumerate(((raw_q, hi), (raw_g, hi), (raw_q, lo), (raw_g, lo))):
        by_chunk(q_own, i, raw[pl.ds(place, SPAN)])
    for i, (raw, place) in enumerate(((raw_k, lo), (raw_v, lo), (raw_k, hi), (raw_v, hi))):
        by_chunk(kv_own, i, raw[pl.ds(place, SPAN)])

    def remote(src, dst, send, recv, device):
        return pltpu.make_async_remote_copy(
            src_ref=src, dst_ref=dst, send_sem=send, recv_sem=recv, device_id=device, device_id_type=MESH
        )

    order = [lax.rem(h + step, chunks) for step in range(1, chunks + 1)]
    kv_copy = remote(kv_own, kv_mate, kv_sem.at[0], kv_sem.at[1], mate)
    q_copies = [
        remote(q_own.at[j], q_far[j], far_sem.at[0, j], far_sem.at[1, j], {"ctx": behind}) for j in range(chunks)
    ]
    kv_copies = [
        remote(kv_own.at[order[j]], kv_far[j], far_sem.at[0, j], far_sem.at[1, j], {"ctx": ahead})
        for j in range(chunks)
    ]
    row_copies = [
        remote(own, far, row_sem.at[0, i], row_sem.at[1, i], {"ctx": behind})
        for i, (own, far) in enumerate(((norm_own, norm_far), (delta_own, delta_far)))
    ]
    dq_copies = [
        remote(next_out.at[j], dq_part[j], dq_sem.at[0, j], dq_sem.at[1, j], {"ctx": ahead}) for j in range(chunks)
    ]
    back_copies = [
        remote(back_out.at[j], back_part[j], back_sem.at[0, j], back_sem.at[1, j], {"ctx": behind})
        for j in range(chunks)
    ]
    mate_copy = remote(mate_out, mate_part, mate_sem.at[0], mate_sem.at[1], mate)
    starts_line = jnp.logical_and(even, start_of_line)

    def send_chunk(j):
        pl.when(odd)(kv_copies[j].start)
        pl.when(wants_behind)(q_copies[j].start)

    send_chunk(0)
    kv_copy.start()

    for copy in loads[5:]:
        copy.wait()
    for i, place in enumerate((hi, lo)):
        norm_own[:, pl.ds(i * SPAN, SPAN)] = raw_norm[:, pl.ds(place, SPAN)] * LOG2E
        product = raw_g[pl.ds(place, SPAN)].astype(F32) * raw_o[pl.ds(place, SPAN)].astype(F32)
        delta_own[:, pl.ds(i * SPAN, SPAN)] = jnp.sum(product.T, axis=0, keepdims=True)

    def send_rows():
        for copy in row_copies:
            copy.start()

    pl.when(wants_behind)(send_rows)

    def either(a, b):
        return a + b - 2 * a * b

    def at(i, size):
        return pl.ds(i * size, size)

    def whole(ref, i):
        return ref[:, at(i, each)].reshape(SPAN, DIM)

    def block(qpart, kv, kvpart, diagonal=False):
        return tile(
            whole(q_own, 2 * qpart),
            whole(q_own, 2 * qpart + 1),
            norm_own[:, at(qpart, SPAN)],
            delta_own[:, at(qpart, SPAN)],
            whole(kv, 2 * kvpart),
            whole(kv, 2 * kvpart + 1),
            diagonal,
        )

    top, bottom = pl.ds(0, SPAN), pl.ds(SPAN, SPAN)

    dq, dk, dv = block(0, kv_own, 0)
    dq_acc[top] = dq
    dk_acc[0, top] = dk
    dv_acc[0, top] = dv
    send_chunk(1)
    dq, dk, dv = block(1, kv_own, 0, True)
    dq_acc[bottom] = dq
    dk_acc[0, top] += dk
    dv_acc[0, top] += dv
    send_chunk(2)
    dq, dk, dv = block(0, kv_own, 1, True)
    dq_acc[top] += dq
    dk_acc[0, bottom] = dk
    dv_acc[0, bottom] = dv
    send_chunk(3)

    @pl.when(jnp.logical_and(is_even_place, wants_behind))
    def _():
        pl.semaphore_wait(hello.at[0], 1)

    @pl.when(is_even_place)
    def _():
        pl.semaphore_wait(barrier, heads - 1)
        tell_heads(relay)

    @pl.when(starts_line)
    def _():
        pl.semaphore_wait(hello.at[1], 1)
        q_copies[0].start()
        send_rows()

    def tell_ahead():
        @pl.when(is_even_place)
        def _():
            pl.semaphore_wait(relay, heads - 1)
            tell(plane, ctx=ahead)

    for ref in (dq_end, dk_end, dv_end):
        for pair in range(2):
            ref[pair, bottom] = jnp.zeros((SPAN, DIM), F32)

    def if_low(pair, part, end, on=1):
        return end[pair, at(1 - on * either(lows[pair], part), SPAN)]

    def split(pair, value):
        is_low = jnp.full(value.shape, lows[pair], jnp.int32) == 1
        return jnp.where(is_low, value, 0.0), jnp.where(is_low, 0.0, value)

    def send_mate():
        for part in range(2):
            for i, (acc, end, factor) in enumerate(((dk_acc, dk_end, SCALE), (dv_acc, dv_end, 1.0))):
                value = if_low(0, part, end)
                if part == 0:
                    value += acc[1, top]
                mate_out[pl.ds(part * TOK + i * SPAN, SPAN)] = (value * factor).astype(BF16)
        mate_copy.start()

    def add(ref, index, value, first):
        ref[index] = value if first else ref[index] + value

    @pl.when(even)
    def _():
        kv_copy.wait_recv()
        for copy in row_copies:
            copy.wait_recv()
        tell_ahead()
        for j in range(chunks):
            if j + 1 < chunks:
                pl.when(starts_line)(q_copies[j + 1].start)
            q_copies[j].wait_recv()
            q = q_far[j]
            dq_hi = dq_lo = 0.0
            for pair, kv, slot in ((0, kv_mate, 1), (1, kv_own, 0)):
                row = pl.ds(j * each, each)
                dq, dk, dv = tile(
                    q[at(0, each)], q[at(1, each)], norm_far[:, row], delta_far[:, row], whole(kv, 0), whole(kv, 1)
                )
                dq_hi += dq
                add(dk_acc, (slot, top), dk, j == 0 and slot == 1)
                add(dv_acc, (slot, top), dv, j == 0 and slot == 1)
                is_low = lows[pair]
                row = pl.ds(is_low * SPAN + j * each, each)
                dq, dk, dv = tile(
                    q[at(2 * is_low, each)],
                    q[at(2 * is_low + 1, each)],
                    norm_far[:, row],
                    delta_far[:, row],
                    whole(kv, 2 * (1 - is_low)),
                    whole(kv, 2 * (1 - is_low) + 1),
                )
                to_lo, to_hi = split(pair, dq)
                dq_lo += to_lo
                dq_hi += to_hi
                add(dk_end, (pair, top), dk, j == 0)
                add(dv_end, (pair, top), dv, j == 0)
            next_out[j, at(0, each)] = (dq_hi * SCALE).astype(BF16)
            next_out[j, at(1, each)] = (dq_lo * SCALE).astype(BF16)
            dq_copies[j].start()
        send_mate()

    @pl.when(odd)
    def _():
        kv_copy.wait_recv()
        dq, dk, dv = block(0, kv_mate, 0)
        dq_acc[top] += dq
        dk_acc[1, top] = dk
        dv_acc[1, top] = dv
        dq, dk, dv = block(lows[0], kv_mate, 1 - lows[0])
        dq_end[0, top] = dq
        dk_end[0, top] = dk
        dv_end[0, top] = dv
        send_mate()
        tell_ahead()

    low_of = [low_place, 1 - low_place]

    def visit_behind():
        @pl.when(is_even_place)
        def _():
            pl.semaphore_wait(hello.at[1], 1)

        is_low = lows[1]
        for j in range(chunks):
            kv_copies[j].wait_recv()
            kv = kv_far[j]
            dq, dk, dv = tile(
                whole(q_own, 0), whole(q_own, 1), norm_own[:, top], delta_own[:, top], kv[at(0, each)], kv[at(1, each)]
            )
            dq_acc[top] += dq
            dq, dk_end_j, dv_end_j = tile(
                whole(q_own, 2 * is_low),
                whole(q_own, 2 * is_low + 1),
                norm_own[:, at(is_low, SPAN)],
                delta_own[:, at(is_low, SPAN)],
                kv[at(2 * (1 - is_low), each)],
                kv[at(2 * (1 - is_low) + 1, each)],
            )
            add(dq_end, (1, top), dq, j == 0)
            for i, (value, end, factor) in enumerate(((dk, dk_end_j, SCALE), (dv, dv_end_j, 1.0))):
                to_lo, to_hi = split(1, end)
                back_out[j, at(i, each)] = ((value + to_lo) * factor).astype(BF16)
                back_out[j, at(2 + i, each)] = (to_hi * factor).astype(BF16)
            back_copies[j].start()
        for p in range(2):
            value = dq_acc[at(1 - low_of[p], SPAN)]
            value += if_low(0, low_of[p], dq_end) + if_low(1, low_of[p], dq_end)
            dq_out[pl.ds(p * SPAN, SPAN)] = (value * SCALE).astype(BF16)

    pl.when(jnp.logical_and(odd, jnp.logical_not(start_of_line)))(visit_behind)

    mate_copy.wait_recv()

    @pl.when(is_odd_place)
    def _():
        pl.semaphore_wait(plane, 1)

    def own_copy(to):
        return remote(own_out.at[to], own_part.at[h], own_send.at[to], own_recv.at[h], {"head": to})

    for j, r in enumerate(order):
        pl.when(odd)(back_copies[j].wait_recv)
        for p in range(2):
            part = low_of[p]
            to = p * chunks + r
            row = r * each

            def rows_of(i):
                return pl.ds(i * SPAN + row, each)

            halves = []
            for i, (acc, end, factor) in enumerate(((dk_acc, dk_end, SCALE), (dv_acc, dv_end, 1.0))):
                more = end[1, rows_of(1 - (1 - side) * either(lows[1], part))]
                value = (acc[0, rows_of(part)] + more) * factor
                halves.append(value + mate_part[rows_of(2 * part + i)].astype(F32))

            @pl.when(even)
            def _():
                for i in range(2):
                    own_out[to, at(i, each)] = halves[i].astype(BF16)

            @pl.when(odd)
            def _():
                for i in range(2):
                    back = back_part[j][at(2 * part + i, each)].astype(F32)
                    own_out[to, at(i, each)] = (halves[i] + back).astype(BF16)

            if j < chunks - 1:
                own_copy(to).start()
            else:
                pl.when(to != h)(own_copy(to).start)
    own_part[h] = own_out[h]

    pl.when(jnp.logical_and(odd, start_of_line))(visit_behind)

    def finish_queries():
        for j in range(chunks):
            dq_copies[j].wait_recv()
            for p in range(2):
                place = 1 - low_of[p]
                own = dq_acc[pl.ds(place * SPAN + j * each, each)] * SCALE
                far = dq_part[j][at(place, each)].astype(F32)
                dq_out[pl.ds(p * SPAN + j * each, each)] = (own + far).astype(BF16)

    pl.when(wants_behind)(finish_queries)

    for step in range(1, heads):
        sender = lax.rem(h + step, heads)
        remote(own_out.at[sender], own_part.at[sender], own_send.at[sender], own_recv.at[sender], mate).wait_recv()
    total = own_part[0].astype(F32)
    for i in range(1, heads):
        total += own_part[i].astype(F32)
    dkv_out[...] = total.astype(BF16)
    pl.when(starts_line)(finish_queries)

    kv_copy.wait_send()
    mate_copy.wait_send()
    for step in range(1, heads):
        own_copy(lax.rem(h + step, heads)).wait_send()

    @pl.when(even)
    def _():
        for copy in (*row_copies, *q_copies, *dq_copies):
            copy.wait_send()

    @pl.when(odd)
    def _():
        for copy in (*kv_copies, *back_copies):
            copy.wait_send()


def local(queries, keys, values, outputs, out_grad, log_norm, span_ids):
    holders, heads = lax.axis_size("ctx"), lax.axis_size("head")
    each, chunks = TOK // heads, heads // 2
    flat = lambda a: a.reshape(TOK, DIM)
    body = lambda *refs: kernel(holders, heads, *refs)
    dma = pltpu.SemaphoreType.DMA
    dq, dkv = pl.pallas_call(
        body,
        out_shape=[
            pltpu.VMEM((TOK, DIM), BF16),
            pltpu.VMEM((2 * each, DIM), BF16),
        ],
        in_specs=[
            *[pl.BlockSpec(memory_space=pltpu.HBM)] * 7,
        ],
        out_specs=[pl.BlockSpec(memory_space=pltpu.VMEM)] * 2,
        scratch_shapes=[
            pltpu.SMEM((2 * holders,), jnp.int32),
            pltpu.VMEM((1, TOK), F32),
            *[pltpu.VMEM((TOK, DIM), BF16)] * 5,
            *[pltpu.VMEM((chunks, 4 * each, DIM), BF16)] * 3,
            *[pltpu.VMEM((4 * each, DIM), BF16)] * (2 * chunks),
            *[pltpu.VMEM((2 * each, DIM), BF16)] * chunks,
            *[pltpu.VMEM((4 * each, DIM), BF16)] * chunks,
            *[pltpu.VMEM((1, TOK), F32)] * 4,
            pltpu.VMEM((TOK, DIM), F32),
            *[pltpu.VMEM((2, TOK, DIM), F32)] * 5,
            pltpu.VMEM((2 * TOK, DIM), BF16),
            pltpu.VMEM((2 * TOK, DIM), BF16),
            pltpu.VMEM((chunks, 2 * each, DIM), BF16),
            pltpu.VMEM((chunks, 4 * each, DIM), BF16),
            pltpu.VMEM((heads, 2 * each, DIM), BF16),
            pltpu.VMEM((heads, 2 * each, DIM), BF16),
            dma((7,)),
            dma((2,)),
            dma((2,)),
            dma((2, chunks)),
            dma((2, 2)),
            dma((2, chunks)),
            dma((2, chunks)),
            dma((heads,)),
            dma((heads,)),
            pltpu.SemaphoreType.REGULAR((2,)),
            pltpu.SemaphoreType.REGULAR,
            pltpu.SemaphoreType.REGULAR,
        ],
        compiler_params=pltpu.CompilerParams(
            collective_id=0, has_side_effects=True, vmem_limit_bytes=VMEM_GRANT
        ),
    )(
        span_ids,
        flat(queries),
        flat(out_grad),
        flat(outputs),
        keys,
        values,
        log_norm,
    )
    return dq.reshape(queries.shape), dkv[:each], dkv[each:]


def solution(mesh):
    in_specs = (
        P("ctx", "head", None),
        P("ctx", None),
        P("ctx", None),
        P("ctx", "head", None),
        P("ctx", "head", None),
        P("head", "ctx"),
        P(),
    )
    out_specs = (P("ctx", "head", None), P(("ctx", "head"), None), P(("ctx", "head"), None))
    return jax.shard_map(local, mesh=mesh, in_specs=in_specs, out_specs=out_specs, check_vma=False)
```

time: 35.2 us -> 34.3 us (0.974)
  the two profiles are of different devices: /device:TPU:6 before, /device:TPU:1 now
where the time goes in v4:
time: 34.3 us; the launch traced here: 34.2 us
  Pallas kernels  32.2 us (94%)
  local copies, waits for them, and re-layouts  1.33 us (4%)
  between operations  0.64 us (2%)
    pallas_call x1, Pallas kernels, local(): pl.pallas_call(body, out_shape=[pltpu.VMEM((TOK, DIM), BF16), pltpu.VMEM(...  32.2 us
    unnamed x1, local copies, waits for them, and re-layouts  0.71 us

profile of v4, /device:TPU:1, one launch (start us, length us, event | category | flops | bytes accessed | tf_op | source)
XLA Modules:
  0.0 34.2 jit_solution(1475514420552259146)
XLA Ops:
  0.6 32.2 %shard_map.94 = (bf16[1024,128]{1,0:T(8,128)(2,1)S(1)}, bf16[256,128]{1,0:T(8,128)(2,1)S(1)}) custom-call(s32[128]{0:T(128)} %refs_0_.1, bf16[1024,128]{1,0:T(8,128)(2,1)} %bitcast.5, bf16[1024,128]{1,0:T(8,128)(2,1)} %bitcast.6, bf16[1024,128]{1,0:T(8,128)(2,1)} %bitcast.7, bf16[1024,128]{1,0:T(8,128)(2,1)} %refs_4_.1, bf16[1024,128]{1,0:T(8,128)(2,1)} %refs_5_.1, ...), custom_call_target="tpu_custom_call" | custom-call | tf_op jit(solution)/shard_map/pallas_call | solution.py:448
  32.8 0.7 %copy.11 = bf16[1024,1,128]{2,0,1:T(8,128)(2,1)} copy(bf16[1024,1,128]{2,0,1:T(8,128)(2,1)S(1)} %bitcast.4) | data formatting | bytes 524288
  33.5 0.6 %fusion = (bf16[128,128]{1,0:T(8,128)(2,1)}, bf16[128,128]{1,0:T(8,128)(2,1)}) fusion(bf16[256,128]{1,0:T(8,128)(2,1)S(1)} %get-tuple-element.6), kind=kLoop, calls=%fused_computation | loop fusion | bytes 131072 | tf_op jit(solution)/shard_map/slice | solution.py:500

commit v5 on v4

--- a/solution.py
+++ b/solution.py
@@ -234,11 +234,11 @@
         pl.semaphore_wait(barrier, heads - 1)
         tell_heads(relay)
 
-    @pl.when(starts_line)
-    def _():
+    def hear_behind():
         pl.semaphore_wait(hello.at[1], 1)
         q_copies[0].start()
         send_rows()
+        q_copies[1].start()
 
     def tell_ahead():
         @pl.when(is_even_place)
@@ -276,8 +276,10 @@
             copy.wait_recv()
         tell_ahead()
         for j in range(chunks):
-            if j + 1 < chunks:
-                pl.when(starts_line)(q_copies[j + 1].start)
+            if j == 2:
+                pl.when(starts_line)(hear_behind)
+            if j == 2 + 1:
+                pl.when(starts_line)(q_copies[2].start)
             q_copies[j].wait_recv()
             q = q_far[j]
             dq_hi = dq_lo = 0.0
@@ -307,6 +309,7 @@
             next_out[j, at(0, each)] = (dq_hi * SCALE).astype(BF16)
             next_out[j, at(1, each)] = (dq_lo * SCALE).astype(BF16)
             dq_copies[j].start()
+        pl.when(starts_line)(q_copies[3].start)
         send_mate()
 
     @pl.when(odd)

time: 34.3 us -> 33.1 us (0.965)
  Pallas kernels: 32.2 us -> 30.6 us
    pallas_call x1, Pallas kernels: 32.2 us -> 30.6 us  [local(): pl.pallas_call(body, out_shape=[pltpu.VMEM((TOK, DIM), BF16), pltpu.VMEM(...]
where the time goes in v5:
time: 33.1 us; the launch traced here: 32.6 us
  Pallas kernels  30.6 us (92%)
  local copies, waits for them, and re-layouts  1.33 us (4%)
  between operations  0.64 us (2%)
    pallas_call x1, Pallas kernels, local(): pl.pallas_call(body, out_shape=[pltpu.VMEM((TOK, DIM), BF16), pltpu.VMEM(...  30.6 us
    unnamed x1, local copies, waits for them, and re-layouts  0.71 us

profile of v5, /device:TPU:1, one launch (start us, length us, event | category | flops | bytes accessed | tf_op | source)
XLA Modules:
  0.0 32.6 jit_solution(17640504276980381493)
XLA Ops:
  0.6 30.6 %shard_map.94 = (bf16[1024,128]{1,0:T(8,128)(2,1)S(1)}, bf16[256,128]{1,0:T(8,128)(2,1)S(1)}) custom-call(s32[128]{0:T(128)} %refs_0_.1, bf16[1024,128]{1,0:T(8,128)(2,1)} %bitcast.5, bf16[1024,128]{1,0:T(8,128)(2,1)} %bitcast.6, bf16[1024,128]{1,0:T(8,128)(2,1)} %bitcast.7, bf16[1024,128]{1,0:T(8,128)(2,1)} %refs_4_.1, bf16[1024,128]{1,0:T(8,128)(2,1)} %refs_5_.1, ...), custom_call_target="tpu_custom_call" | custom-call | tf_op jit(solution)/shard_map/pallas_call | solution.py:451
  31.3 0.7 %copy.11 = bf16[1024,1,128]{2,0,1:T(8,128)(2,1)} copy(bf16[1024,1,128]{2,0,1:T(8,128)(2,1)S(1)} %bitcast.4) | data formatting | bytes 524288
  32.0 0.6 %fusion = (bf16[128,128]{1,0:T(8,128)(2,1)}, bf16[128,128]{1,0:T(8,128)(2,1)}) fusion(bf16[256,128]{1,0:T(8,128)(2,1)S(1)} %get-tuple-element.6), kind=kLoop, calls=%fused_computation | loop fusion | bytes 131072 | tf_op jit(solution)/shard_map/slice | solution.py:503

commit v6 on v5

--- a/solution.py
+++ b/solution.py
@@ -39,13 +39,13 @@
     *rest,
 ):
     chunks = heads // 2
-    q_far, kv_far, dq_part, back_part = (rest[i * chunks : (i + 1) * chunks] for i in range(4))
+    q_far, kv_far, dq_part, back_part, mate_part = (rest[i * chunks : (i + 1) * chunks] for i in range(5))
     (
         norm_own, norm_far, delta_own, delta_far, dq_acc, dk_acc, dv_acc, dq_end, dk_end, dv_end,
-        mate_out, mate_part, next_out, back_out, own_out, own_part,
+        mate_out, next_out, back_out, own_out, own_part,
         load_sem, kv_sem, mate_sem, far_sem, row_sem, dq_sem, back_sem, own_send, own_recv,
         hello, relay, plane,
-    ) = rest[4 * chunks :]
+    ) = rest[5 * chunks :]
     each = TOK // heads
     c = lax.axis_index("ctx")
     h = lax.axis_index("head")
@@ -164,7 +164,9 @@
         remote(back_out.at[j], back_part[j], back_sem.at[0, j], back_sem.at[1, j], {"ctx": behind})
         for j in range(chunks)
     ]
-    mate_copy = remote(mate_out, mate_part, mate_sem.at[0], mate_sem.at[1], mate)
+    mate_copies = [
+        remote(mate_out.at[j], mate_part[j], mate_sem.at[0, j], mate_sem.at[1, j], mate) for j in range(chunks)
+    ]
     starts_line = jnp.logical_and(even, start_of_line)
 
     def send_chunk(j):
@@ -258,13 +260,14 @@
         return jnp.where(is_low, value, 0.0), jnp.where(is_low, 0.0, value)
 
     def send_mate():
-        for part in range(2):
-            for i, (acc, end, factor) in enumerate(((dk_acc, dk_end, SCALE), (dv_acc, dv_end, 1.0))):
-                value = if_low(0, part, end)
-                if part == 0:
-                    value += acc[1, top]
-                mate_out[pl.ds(part * TOK + i * SPAN, SPAN)] = (value * factor).astype(BF16)
-        mate_copy.start()
+        for j, r in enumerate(order):
+            for part in range(2):
+                for i, (acc, end, factor) in enumerate(((dk_acc, dk_end, SCALE), (dv_acc, dv_end, 1.0))):
+                    value = end[0, pl.ds((1 - either(lows[0], part)) * SPAN + r * each, each)]
+                    if part == 0:
+                        value += acc[1, pl.ds(r * each, each)]
+                    mate_out[j, at(2 * part + i, each)] = (value * factor).astype(BF16)
+            mate_copies[j].start()
 
     def add(ref, index, value, first):
         ref[index] = value if first else ref[index] + value
@@ -362,8 +365,6 @@
 
     pl.when(jnp.logical_and(odd, jnp.logical_not(start_of_line)))(visit_behind)
 
-    mate_copy.wait_recv()
-
     @pl.when(is_odd_place)
     def _():
         pl.semaphore_wait(plane, 1)
@@ -372,6 +373,7 @@
         return remote(own_out.at[to], own_part.at[h], own_send.at[to], own_recv.at[h], {"head": to})
 
     for j, r in enumerate(order):
+        mate_copies[j].wait_recv()
         pl.when(odd)(back_copies[j].wait_recv)
         for p in range(2):
             part = low_of[p]
@@ -385,7 +387,7 @@
             for i, (acc, end, factor) in enumerate(((dk_acc, dk_end, SCALE), (dv_acc, dv_end, 1.0))):
                 more = end[1, rows_of(1 - (1 - side) * either(lows[1], part))]
                 value = (acc[0, rows_of(part)] + more) * factor
-                halves.append(value + mate_part[rows_of(2 * part + i)].astype(F32))
+                halves.append(value + mate_part[j][at(2 * part + i, each)].astype(F32))
 
             @pl.when(even)
             def _():
@@ -427,7 +429,8 @@
     pl.when(starts_line)(finish_queries)
 
     kv_copy.wait_send()
-    mate_copy.wait_send()
+    for copy in mate_copies:
+        copy.wait_send()
     for step in range(1, heads):
         own_copy(lax.rem(h + step, heads)).wait_send()
 
@@ -465,19 +468,18 @@
             *[pltpu.VMEM((chunks, 4 * each, DIM), BF16)] * 3,
             *[pltpu.VMEM((4 * each, DIM), BF16)] * (2 * chunks),
             *[pltpu.VMEM((2 * each, DIM), BF16)] * chunks,
-            *[pltpu.VMEM((4 * each, DIM), BF16)] * chunks,
+            *[pltpu.VMEM((4 * each, DIM), BF16)] * (2 * chunks),
             *[pltpu.VMEM((1, TOK), F32)] * 4,
             pltpu.VMEM((TOK, DIM), F32),
             *[pltpu.VMEM((2, TOK, DIM), F32)] * 5,
-            pltpu.VMEM((2 * TOK, DIM), BF16),
-            pltpu.VMEM((2 * TOK, DIM), BF16),
+            pltpu.VMEM((chunks, 4 * each, DIM), BF16),
             pltpu.VMEM((chunks, 2 * each, DIM), BF16),
             pltpu.VMEM((chunks, 4 * each, DIM), BF16),
             pltpu.VMEM((heads, 2 * each, DIM), BF16),
             pltpu.VMEM((heads, 2 * each, DIM), BF16),
             dma((7,)),
             dma((2,)),
-            dma((2,)),
+            dma((2, chunks)),
             dma((2, chunks)),
             dma((2, 2)),
             dma((2, chunks)),

time: 33.1 us -> 33.5 us (1.012)
  the two profiles are of different devices: /device:TPU:1 before, /device:TPU:8 now
where the time goes in v6:
time: 33.5 us; the launch traced here: 33.4 us
  Pallas kernels  31.4 us (94%)
  local copies, waits for them, and re-layouts  1.33 us (4%)
  between operations  0.64 us (2%)
    pallas_call x1, Pallas kernels, local(): pl.pallas_call(body, out_shape=[pltpu.VMEM((TOK, DIM), BF16), pltpu.VMEM(...  31.4 us
    unnamed x1, local copies, waits for them, and re-layouts  0.71 us

profile of v6, /device:TPU:8, one launch (start us, length us, event | category | flops | bytes accessed | tf_op | source)
XLA Modules:
  0.0 33.4 jit_solution(10698407507464915794)
XLA Ops:
  0.6 31.4 %shard_map.94 = (bf16[1024,128]{1,0:T(8,128)(2,1)S(1)}, bf16[256,128]{1,0:T(8,128)(2,1)S(1)}) custom-call(s32[128]{0:T(128)} %refs_0_.1, bf16[1024,128]{1,0:T(8,128)(2,1)} %bitcast.5, bf16[1024,128]{1,0:T(8,128)(2,1)} %bitcast.6, bf16[1024,128]{1,0:T(8,128)(2,1)} %bitcast.7, bf16[1024,128]{1,0:T(8,128)(2,1)} %refs_4_.1, bf16[1024,128]{1,0:T(8,128)(2,1)} %refs_5_.1, ...), custom_call_target="tpu_custom_call" | custom-call | tf_op jit(solution)/shard_map/pallas_call | solution.py:454
  32.1 0.7 %copy.11 = bf16[1024,1,128]{2,0,1:T(8,128)(2,1)} copy(bf16[1024,1,128]{2,0,1:T(8,128)(2,1)S(1)} %bitcast.4) | data formatting | bytes 524288
  32.8 0.6 %fusion = (bf16[128,128]{1,0:T(8,128)(2,1)}, bf16[128,128]{1,0:T(8,128)(2,1)}) fusion(bf16[256,128]{1,0:T(8,128)(2,1)S(1)} %get-tuple-element.6), kind=kLoop, calls=%fused_computation | loop fusion | bytes 131072 | tf_op jit(solution)/shard_map/slice | solution.py:505
